TPU v7x, 32 devices: a whole 2x2x4 slice. The times are simulated.
32 devices in a mesh: section: 2 (over x), dp: 4 (over y, core), tensor: 4 (over z).
Axes of the slice: x: 2, y: 2, z: 4, core: 2. Of those that a mesh axis runs over, the one named last changes fastest.
Arguments:
- boundary: bfloat16 [2, 4, 1024, 4, 640], P('section', None, 'tensor', 'dp'), may hold values from -6 to 6
- positions: int32 [4, 1024, 4], P(None, None, 'dp'), may hold values from 0 to 1023, as said below
- w_query: bfloat16 [2, 640, 1024], P('section', 'dp', 'tensor'), may hold values from -0.25 to 0.25
- w_keyval: bfloat16 [2, 640, 512], P('section', 'dp', 'tensor'), may hold values from -0.25 to 0.25
- w_out: bfloat16 [2, 1024, 640], P('section', 'tensor', 'dp'), may hold values from -0.1875 to 0.1875
- w_gateup: bfloat16 [2, 640, 2, 2048], P('section', 'dp', None, 'tensor'), may hold values from -0.25 to 0.25
- down_weight: bfloat16 [2, 2048, 640], P('section', 'tensor', 'dp'), may hold values from -0.125 to 0.125
- norm_gains: float32 [2, 4, 640], P('section'), may hold values from 0.1 to 1.9
- qk_gains: float32 [2, 2, 256], P('section'), may hold values from 0.1 to 1.9
Outputs:
- ends: float32 [2, 4, 1024, 4, 640], P('section', None, 'tensor', 'dp')
- grad_query: float32 [2, 640, 1024], P('section', 'dp', 'tensor')
- grad_keyval: float32 [2, 640, 512], P('section', 'dp', 'tensor')
- grad_out: float32 [2, 1024, 640], P('section', 'tensor', 'dp')
- grad_gateup: float32 [2, 640, 2, 2048], P('section', 'dp', None, 'tensor')
- grad_down: float32 [2, 2048, 640], P('section', 'tensor', 'dp')
- grad_norm_gains: float32 [2, 4, 640], P('section')
- grad_qk_gains: float32 [2, 2, 256], P('section')
Inputs may be any that keep to these rules, and one draw needn't show every extreme that they name: `positions`: sequences are packed with whole documents in order; a document begins where the position is 0 (always at a sequence's first token) and counts up by one; every sequence holds one document of 832 tokens or more.
All inputs are finite; a program needn't handle non-finite values.
Results may differ from a plain program's by a relative error of at most 0.035.
Values may be sent and summed in bfloat16 or wider, within the bound.
A program may use at most 192 MiB of HBM per device.

v0:
```python
import jax
import jax.numpy as jnp
from jax import lax
from jax.sharding import PartitionSpec as P

HD = 256
WIN = 512
LEN = 1024


epsilon = 1e-06


def passed_along(shard, axis, by):
    peers = lax.axis_size(axis)
    pairs = [(i, i + by) for i in range(peers) if 0 <= i + by < peers]
    return lax.ppermute(shard, axis, pairs)


def rms_scale(rows, gain):
    return rows * lax.rsqrt(jnp.mean(rows * rows, axis=-1, keepdims=True) + epsilon) * gain


def rotary_angles(places, base, width):
    freqs = jnp.exp(-jnp.log(base) * jnp.arange(width // 2, dtype=jnp.float32) * (2.0 / width))
    return places.astype(jnp.float32)[..., None] * freqs


def rotary(values, angles):
    half = values.shape[-1] // 2
    front, back = (values[..., :half], values[..., half:])
    cosine, sine = (jnp.cos(angles), jnp.sin(angles))
    return jnp.concatenate([front * cosine - back * sine, back * cosine + front * sine], axis=-1)


def qk_piece(query_raw, key_raw, query_gain, key_gain, angles):
    query = rotary(rms_scale(query_raw, query_gain), angles[:, :, None])
    keys = rotary(rms_scale(key_raw, key_gain), angles)
    return (query, keys)


def gated(gate, up):
    return jax.nn.gelu(gate, approximate=True) * up


def collect(rows):
    return lax.all_gather(rows, "tensor", axis=0, tiled=True)


def spread_total_sum(terms):
    total = 0.0
    for left, weight, pattern in terms:
        total = total + jnp.einsum(pattern, left, weight, preferred_element_type=jnp.float32)
    return lax.psum_scatter(
        total.astype(jnp.bfloat16), "tensor", scatter_dimension=0, tiled=True
    ).astype(jnp.float32)


def split_blocks(array, block):
    return array.reshape((array.shape[0] // block, block) + array.shape[1:])


def allowed_mask(block_pos, block_doc, places, documents, window):
    query_pos = block_pos.T[:, :, None]
    key_pos = places.T[:, None, :]
    same = block_doc.T[:, :, None] == documents.T[:, None, :]
    return same & (key_pos <= query_pos) & (query_pos - key_pos < window)


def block_scores(query_block, keys, mask):
    scale = query_block.shape[-1] ** (-0.5)
    scores = (
        jnp.einsum("qshd,ksd->shqk", query_block, keys, preferred_element_type=jnp.float32) * scale
    )
    return jnp.where(mask[:, None], scores, -1e30)


def attend_forward(query, keys, values, places, window):
    block = min(512, query.shape[0])
    documents = jnp.cumsum((places == 0).astype(jnp.int32), axis=0)

    def one_block(args):
        query_block, block_pos, block_doc = args
        scores = block_scores(
            query_block, keys, allowed_mask(block_pos, block_doc, places, documents, window)
        )
        peak = jnp.max(scores, axis=-1, keepdims=True)
        weights = jnp.exp(scores - peak)
        totals = jnp.sum(weights, axis=-1, keepdims=True)
        probs = (weights / totals).astype(jnp.bfloat16)
        mixed = jnp.einsum("shqk,ksd->qshd", probs, values, preferred_element_type=jnp.float32)
        return (mixed, peak[..., 0] + jnp.log(totals[..., 0]))

    mixed, logsum = lax.map(
        one_block,
        (split_blocks(query, block), split_blocks(places, block), split_blocks(documents, block)),
    )
    return (mixed.reshape(query.shape), logsum)


def attend_backward(query, keys, values, places, window, logsum, grad_mixed):
    block = min(512, query.shape[0])
    scale = query.shape[-1] ** (-0.5)
    documents = jnp.cumsum((places == 0).astype(jnp.int32), axis=0)

    def one_block(carry, args):
        grad_keys, grad_values = carry
        query_block, block_pos, block_doc, block_sum, grad_block = args
        scores = block_scores(
            query_block, keys, allowed_mask(block_pos, block_doc, places, documents, window)
        )
        probs = jnp.exp(scores - block_sum[..., None])
        grad_probs = jnp.einsum(
            "qshd,ksd->shqk", grad_block, values, preferred_element_type=jnp.float32
        )
        inner = jnp.sum(probs * grad_probs, axis=-1, keepdims=True)
        grad_scores = (probs * (grad_probs - inner)).astype(jnp.bfloat16)
        grad_query = (
            jnp.einsum("shqk,ksd->qshd", grad_scores, keys, preferred_element_type=jnp.float32)
            * scale
        )
        grad_keys = (
            grad_keys
            + jnp.einsum(
                "shqk,qshd->ksd", grad_scores, query_block, preferred_element_type=jnp.float32
            )
            * scale
        )
        grad_values = grad_values + jnp.einsum(
            "shqk,qshd->ksd",
            probs.astype(jnp.bfloat16),
            grad_block,
            preferred_element_type=jnp.float32,
        )
        return ((grad_keys, grad_values), grad_query)

    zeros = jnp.zeros(keys.shape, jnp.float32)
    (grad_keys, grad_values), grad_query = lax.scan(
        one_block,
        (zeros, zeros),
        (
            split_blocks(query, block),
            split_blocks(places, block),
            split_blocks(documents, block),
            logsum,
            split_blocks(grad_mixed, block),
        ),
    )
    return (grad_query.reshape(query.shape), grad_keys, grad_values)


def layer_forward(rows, weights, gains, qk_gain, places, window, base):
    w_query, w_keyval, w_out, w_gateup, down_weight = weights
    normed = rms_scale(rows, gains[0]).astype(jnp.bfloat16)
    normed_all = collect(normed)
    query_raw = jnp.einsum("lsd,de->lse", normed_all, w_query, preferred_element_type=jnp.float32)
    keyval_part = jnp.einsum(
        "lsd,de->lse", normed_all, w_keyval, preferred_element_type=jnp.float32
    ).astype(jnp.bfloat16)
    keyval = lax.all_gather(keyval_part, "tensor", axis=2, tiled=True)
    angles = rotary_angles(places, base, HD)
    query_raw = query_raw.reshape(query_raw.shape[:2] + (query_raw.shape[2] // HD, HD))
    query, keys = qk_piece(
        query_raw, keyval[..., :HD].astype(jnp.float32), qk_gain[0], qk_gain[1], angles
    )
    query = query.astype(jnp.bfloat16)
    keys = keys.astype(jnp.bfloat16)
    mixed, logsum = attend_forward(query, keys, keyval[..., HD:], places, window)
    mixed = mixed.reshape(mixed.shape[:2] + (-1,)).astype(jnp.bfloat16)
    branch = spread_total_sum(((mixed, w_out, "lse,ed->lsd"),))
    middle = rows + rms_scale(branch, gains[1])
    normed_ff = rms_scale(middle, gains[2]).astype(jnp.bfloat16)
    normed_ff_all = collect(normed_ff)
    gateup = jnp.einsum(
        "lsd,dgf->lsgf", normed_ff_all, w_gateup, preferred_element_type=jnp.float32
    )
    hidden_state = gated(gateup[:, :, 0], gateup[:, :, 1]).astype(jnp.bfloat16)
    feedforward_branch = spread_total_sum(((hidden_state, down_weight, "yte,ej->ytj"),))
    output = middle + rms_scale(feedforward_branch, gains[3])
    kept = (
        rows,
        normed_all,
        keyval,
        query_raw,
        query,
        keys,
        mixed,
        logsum,
        branch,
        middle,
        normed_ff_all,
        gateup,
        hidden_state,
        feedforward_branch,
    )
    return (output, kept)


def layer_backward(kept, weights, gains, qk_gain, places, window, base, grad_output):
    (
        rows,
        normed_all,
        keyval,
        query_raw,
        query,
        keys,
        mixed,
        logsum,
        branch,
        middle,
        normed_ff_all,
        gateup,
        hidden_state,
        feedforward_branch,
    ) = kept
    w_query, w_keyval, w_out, w_gateup, down_weight = weights
    _, pull = jax.vjp(rms_scale, feedforward_branch, gains[3])
    grad_branch_ff, grad_gain_post_ff = pull(grad_output)
    feedforward_gradient_total = collect(grad_branch_ff.astype(jnp.bfloat16))
    hidden_state_gradient = jnp.einsum(
        "auv,zv->auz", feedforward_gradient_total, down_weight, preferred_element_type=jnp.float32
    )
    down_weight_gradient = jnp.einsum(
        "yoz,yox->zx", hidden_state, feedforward_gradient_total, preferred_element_type=jnp.float32
    )
    _, pull = jax.vjp(gated, gateup[:, :, 0], gateup[:, :, 1])
    grad_gate, grad_up = pull(hidden_state_gradient)
    grad_gateup = jnp.stack([grad_gate, grad_up], axis=2).astype(jnp.bfloat16)
    grad_w_gateup = jnp.einsum(
        "lsd,lsgf->dgf", normed_ff_all, grad_gateup, preferred_element_type=jnp.float32
    )
    grad_normed_ff = spread_total_sum(((grad_gateup, w_gateup, "lsgf,dgf->lsd"),))
    _, pull = jax.vjp(rms_scale, middle, gains[2])
    grad_middle, grad_gain_pre_ff = pull(grad_normed_ff)
    grad_middle = grad_middle + grad_output
    _, pull = jax.vjp(rms_scale, branch, gains[1])
    grad_branch, grad_gain_post = pull(grad_middle)
    grad_branch_all = collect(grad_branch.astype(jnp.bfloat16))
    grad_mixed = jnp.einsum(
        "lsd,ed->lse", grad_branch_all, w_out, preferred_element_type=jnp.float32
    ).astype(jnp.bfloat16)
    grad_w_out = jnp.einsum(
        "lse,lsd->ed", mixed, grad_branch_all, preferred_element_type=jnp.float32
    )
    grad_query, grad_keys, grad_values = attend_backward(
        query, keys, keyval[..., HD:], places, window, logsum, grad_mixed.reshape(query.shape)
    )
    angles = rotary_angles(places, base, HD)
    _, pull = jax.vjp(
        lambda raw_q, raw_k, gain_q, gain_k: qk_piece(raw_q, raw_k, gain_q, gain_k, angles),
        query_raw,
        keyval[..., :HD].astype(jnp.float32),
        qk_gain[0],
        qk_gain[1],
    )
    grad_query_raw, grad_key_raw, grad_query_gain, grad_key_gain = pull((grad_query, grad_keys))
    grad_keyval = lax.psum_scatter(
        jnp.concatenate([grad_key_raw, grad_values], axis=-1).astype(jnp.bfloat16),
        "tensor",
        scatter_dimension=2,
        tiled=True,
    )
    grad_query_raw = grad_query_raw.reshape(grad_query_raw.shape[:2] + (-1,)).astype(jnp.bfloat16)
    grad_w_query = jnp.einsum(
        "lsd,lse->de", normed_all, grad_query_raw, preferred_element_type=jnp.float32
    )
    grad_w_keyval = jnp.einsum(
        "lsd,lse->de", normed_all, grad_keyval, preferred_element_type=jnp.float32
    )
    grad_normed = spread_total_sum(
        ((grad_query_raw, w_query, "lse,de->lsd"), (grad_keyval, w_keyval, "lse,de->lsd"))
    )
    _, pull = jax.vjp(rms_scale, rows, gains[0])
    grad_rows, grad_gain_pre = pull(grad_normed)
    grad_rows = grad_rows + grad_middle
    grad_weights = (grad_w_query, grad_w_keyval, grad_w_out, grad_w_gateup, down_weight_gradient)
    gain_grads = jnp.stack([grad_gain_pre, grad_gain_post, grad_gain_pre_ff, grad_gain_post_ff])
    qk_grads = jnp.stack([grad_query_gain, grad_key_gain])
    return (grad_rows, grad_weights, gain_grads, qk_grads)


def add_tuples(first_tuple, second_tuple):
    return tuple((left + right for left, right in zip(first_tuple, second_tuple)))


def body(
    boundary, positions, w_query, w_keyval, w_out, w_gateup, down_weight, norm_gains, qk_gains
):
    section = lax.axis_index("section")
    first = section == 0
    window = jnp.where(first, WIN, LEN + 1)
    base = jnp.where(first, 10000.0, 1000000.0).astype(jnp.float32)
    local = boundary[0]
    micro = local.shape[0]
    shards = (w_query[0], w_keyval[0], w_out[0], w_gateup[0], down_weight[0])
    gains = norm_gains[0]
    qk_gain = qk_gains[0]

    def fetch():
        return (
            lax.all_gather(shards[0], "dp", axis=0, tiled=True),
            lax.all_gather(shards[1], "dp", axis=0, tiled=True),
            lax.all_gather(shards[2], "dp", axis=1, tiled=True),
            lax.all_gather(shards[3], "dp", axis=0, tiled=True),
            lax.all_gather(shards[4], "dp", axis=1, tiled=True),
        )

    received = jnp.zeros(local.shape[1:], jnp.bfloat16)
    inputs = []
    results = []
    for tick in range(micro + 1):
        rows = jnp.where(first, local[min(tick, micro - 1)], received).astype(jnp.float32)
        places = lax.dynamic_index_in_dim(
            positions, jnp.clip(tick - section, 0, micro - 1), 0, keepdims=False
        )
        weights = fetch()
        output, kept = layer_forward(rows, weights, gains, qk_gain, places, window, base)
        inputs.append(rows)
        if tick > 0:
            results.append(output)
        if tick < micro:
            received = passed_along(output.astype(jnp.bfloat16), "section", 1)
    pile_rows = jnp.stack(inputs)
    returned = jnp.zeros(local.shape[1:], jnp.bfloat16)
    shard_total = None
    gain_total = jnp.zeros(gains.shape, jnp.float32)
    qk_total = jnp.zeros(qk_gain.shape, jnp.float32)
    sent_back = []
    for tick in range(micro + 1):
        index = tick - 1 + section
        valid = ((index >= 0) & (index < micro)).astype(jnp.float32)
        source = jnp.clip(tick - 1 + 2 * section, 0, micro)
        places = lax.dynamic_index_in_dim(
            positions, jnp.clip(index, 0, micro - 1), 0, keepdims=False
        )
        weights = fetch()
        kept = layer_forward(
            lax.dynamic_index_in_dim(pile_rows, source, 0, keepdims=False),
            weights,
            gains,
            qk_gain,
            places,
            window,
            base,
        )[1]
        grad_in = jnp.where(first, returned, local[min(tick, micro - 1)]).astype(jnp.float32)
        grad_rows, grad_weights, gain_grads, qk_grads = layer_backward(
            kept, weights, gains, qk_gain, places, window, base, grad_in
        )
        grad_weights = tuple((part * valid for part in grad_weights))
        gain_total = gain_total + gain_grads * valid
        qk_total = qk_total + qk_grads * valid
        shares = (
            lax.psum_scatter(
                grad_weights[0].astype(jnp.bfloat16), "dp", scatter_dimension=0, tiled=True
            ).astype(jnp.float32),
            lax.psum_scatter(
                grad_weights[1].astype(jnp.bfloat16), "dp", scatter_dimension=0, tiled=True
            ).astype(jnp.float32),
            lax.psum_scatter(
                grad_weights[2].astype(jnp.bfloat16), "dp", scatter_dimension=1, tiled=True
            ).astype(jnp.float32),
            lax.psum_scatter(
                grad_weights[3].astype(jnp.bfloat16), "dp", scatter_dimension=0, tiled=True
            ).astype(jnp.float32),
            lax.psum_scatter(
                grad_weights[4].astype(jnp.bfloat16), "dp", scatter_dimension=1, tiled=True
            ).astype(jnp.float32),
        )
        shard_total = shares if shard_total is None else add_tuples(shard_total, shares)
        if tick > 0:
            sent_back.append(grad_rows)
        if tick < micro:
            returned = passed_along(grad_rows.astype(jnp.bfloat16), "section", -1)
    gain_total, qk_total = lax.psum((gain_total, qk_total), ("dp", "tensor"))
    ends = jnp.where(first, jnp.stack(sent_back), jnp.stack(results))[None]
    return (
        ends,
        shard_total[0][None],
        shard_total[1][None],
        shard_total[2][None],
        shard_total[3][None],
        shard_total[4][None],
        gain_total[None],
        qk_total[None],
    )


def solution(mesh):
    in_specs = (
        P("section", None, "tensor", "dp", None),
        P(None, None, "dp"),
        P("section", "dp", "tensor"),
        P("section", "dp", "tensor"),
        P("section", "tensor", "dp"),
        P("section", "dp", None, "tensor"),
        P("section", "tensor", "dp"),
        P("section", None, None),
        P("section", None, None),
    )
    out_specs = (
        P("section", None, "tensor", "dp", None),
        P("section", "dp", "tensor"),
        P("section", "dp", "tensor"),
        P("section", "tensor", "dp"),
        P("section", "dp", None, "tensor"),
        P("section", "tensor", "dp"),
        P("section", None, None),
        P("section", None, None),
    )
    return jax.shard_map(body, mesh=mesh, in_specs=in_specs, out_specs=out_specs, check_vma=False)
```

profile of v0, /device:TPU:0, one launch (start us, length us, event | category | flops | bytes accessed | tf_op | source)
XLA Modules:
  0.0 3705.2 jit_solution(18052152569807385640)
XLA Ops:
  170.8 30.4 reduce-scatter.73.cloned.1.call-done
  215.1 32.4 all-gather.61.cloned.1.call-done
  296.0 29.6 reduce-scatter.75.cloned.1.call-done
  330.1 31.5 all-gather.63.cloned.1.call-done
  367.7 30.3 reduce-scatter.77.cloned.1.call-done
  413.6 32.5 all-gather.65.cloned.1.call-done
  494.7 29.6 reduce-scatter.79.cloned.1.call-done
  528.9 31.3 all-gather.67.cloned.1.call-done
  566.3 30.4 reduce-scatter.81.cloned.1.call-done
  612.2 32.5 all-gather.69.cloned.1.call-done
  693.6 29.6 reduce-scatter.83.cloned.1.call-done
  727.7 31.5 all-gather.71.cloned.1.call-done
  812.2 32.2 all-gather.75.cloned.1.call-done
  994.8 31.2 all-gather.77.cloned.1.call-done
  1135.2 31.1 reduce-scatter.91.cloned.1.call-done
  1173.3 31.1 all-gather.81.cloned.1.call-done
  1279.8 29.9 reduce-scatter.93.cloned.1.call-done
  1313.8 31.5 all-gather.73.cloned.1.call-done
  1396.7 29.6 reduce-scatter.95.cloned.1.call-done
  1430.5 31.3 all-gather.83.cloned.1.call-done
  1506.7 30.7 all-gather.85.cloned.1.call-done
  1546.9 30.4 reduce-scatter.99.cloned.1.call-done
  1583.1 31.5 all-gather.115.cloned.1.call-done
  1620.8 30.3 reduce-scatter.129.cloned.1.call-done
  1655.3 31.1 all-gather.87.cloned.1.call-done
  1762.0 29.9 reduce-scatter.101.cloned.1.call-done
  1796.3 31.3 all-gather.89.cloned.1.call-done
  1879.2 29.6 reduce-scatter.103.cloned.1.call-done
  1913.0 31.5 all-gather.91.cloned.1.call-done
  1989.3 30.8 all-gather.93.cloned.1.call-done
  2029.6 30.4 reduce-scatter.107.cloned.1.call-done
  2066.4 31.5 all-gather.95.cloned.1.call-done
  2173.4 29.9 reduce-scatter.109.cloned.1.call-done
  2207.6 31.5 all-gather.97.cloned.1.call-done
  2290.6 29.6 reduce-scatter.111.cloned.1.call-done
  2324.4 31.3 all-gather.99.cloned.1.call-done
  2400.1 31.4 all-gather.101.cloned.1.call-done
  2441.0 30.3 reduce-scatter.115.cloned.1.call-done
  2477.7 31.3 all-gather.103.cloned.1.call-done
  2584.0 29.9 reduce-scatter.117.cloned.1.call-done
  2617.7 31.3 all-gather.105.cloned.1.call-done
  2700.6 29.6 reduce-scatter.119.cloned.1.call-done
  2734.4 31.5 all-gather.107.cloned.1.call-done
  2809.6 31.2 all-gather.109.cloned.1.call-done
  2850.4 30.4 reduce-scatter.123.cloned.1.call-done
  2886.0 31.5 all-gather.111.cloned.1.call-done
  3597.1 32.5 reduce-scatter.125.cloned.1.call-done
  3638.2 59.4 %all-reduce.20 = (f32[1,4,640]{2,1,0:T(4,128)}, f32[1,2,256]{2,1,0:T(2,128)}) all-reduce(f32[1,4,640]{2,1,0:T(4,128)S(1)} %fusion.1256, f32[1,2,256]{2,1,0:T(2,128)S(1)} %fusion.1271), channel_id=1, replica_groups=mesh['section'=2,'dp'=4,'tensor'=4] {'dp','tensor'}, use_global_device_ids=true, to_apply=%region_245.246 | all-reduce | flops 3072 | bytes 24576 | tf_op jit(solution)/shard_map/psum | solution.py:375
  (1616 shorter events, 2349.3 us)
Async XLA Ops:
  50.2 78.7 %reduce-scatter.71.cloned.1.call-start = ((), (), s32[]{:S(2)}) async-start(), calls=%async_computation.61 | async-start | bytes 1638400 | tf_op jit(solution)/shard_map/reduce_scatter | solution.py:54
  170.7 76.8 %all-gather.61.cloned.1.call-start = ((), (), s32[]{:S(2)}) async-start(), calls=%async_computation.64 | async-start | bytes 1638400 | tf_op jit(solution)/shard_map/all_gather | solution.py:47
  250.1 75.5 %reduce-scatter.75.cloned.1.call-start = ((), (), s32[]{:S(2)}) async-start(), calls=%async_computation.65 | async-start | bytes 1638400 | tf_op jit(solution)/shard_map/reduce_scatter | solution.py:54
  367.7 78.4 %all-gather.65.cloned.1.call-start = ((), (), s32[]{:S(2)}) async-start(), calls=%async_computation.68 | async-start | bytes 1638400 | tf_op jit(solution)/shard_map/all_gather | solution.py:47
  448.8 75.6 %reduce-scatter.79.cloned.1.call-start = ((), (), s32[]{:S(2)}) async-start(), calls=%async_computation.69 | async-start | bytes 1638400 | tf_op jit(solution)/shard_map/reduce_scatter | solution.py:54
  566.2 78.5 %all-gather.69.cloned.1.call-start = ((), (), s32[]{:S(2)}) async-start(), calls=%async_computation.72 | async-start | bytes 1638400 | tf_op jit(solution)/shard_map/all_gather | solution.py:47
  647.4 75.8 %reduce-scatter.83.cloned.1.call-start = ((), (), s32[]{:S(2)}) async-start(), calls=%async_computation.73 | async-start | bytes 1638400 | tf_op jit(solution)/shard_map/reduce_scatter | solution.py:54
  764.8 79.6 %all-gather.75.cloned.1.call-start = ((), (), s32[]{:S(2)}) async-start(), calls=%async_computation.77 | async-start | bytes 1638400 | tf_op jit(solution)/shard_map/all_gather | solution.py:47
  812.1 97.4 %all-gather.129.cloned.1.call-start = ((), (), s32[]{:S(2)}) async-start(), calls=%async_computation.151 | async-start | bytes 1310720 | tf_op jit(solution)/shard_map/all_gather | solution.py:160
  847.0 93.1 %all-gather.137.cloned.1.call-start = ((), (), s32[]{:S(2)}) async-start(), calls=%async_computation.155 | async-start | bytes 1310720 | tf_op jit(solution)/shard_map/all_gather | solution.py:160
  880.7 109.9 %reduce-scatter.87.cloned.1.call-start = ((), (), s32[]{:S(2)}) async-start(), calls=%async_computation.78 | async-start | bytes 1638400 | tf_op jit(solution)/shard_map/reduce_scatter | solution.py:54
  1081.9 84.4 %reduce-scatter.91.cloned.1.call-start = ((), (), s32[]{:S(2)}) async-start(), calls=%async_computation.82 | async-start | bytes 1638400 | tf_op jit(solution)/shard_map/reduce_scatter | solution.py:54
  1110.7 93.6 %all-gather.81.cloned.1.call-start = ((), (), s32[]{:S(2)}) async-start(), calls=%async_computation.83 | async-start | bytes 1638400 | tf_op jit(solution)/shard_map/all_gather | solution.py:47
  1173.0 99.7 %reduce-scatter.181.cloned.1.call-start = ((), (), s32[]{:S(2)}) async-start(), calls=%async_computation.156 | async-start | bytes 1310720
  1347.9 78.5 %reduce-scatter.95.cloned.1.call-start = ((), (), s32[]{:S(2)}) async-start(), calls=%async_computation.85 | async-start | bytes 1638400 | tf_op jit(solution)/shard_map/reduce_scatter | solution.py:54
  1655.1 99.7 %reduce-scatter.183.cloned.1.call-start = ((), (), s32[]{:S(2)}) async-start(), calls=%async_computation.157 | async-start | bytes 1310720
  1830.1 78.7 %reduce-scatter.103.cloned.1.call-start = ((), (), s32[]{:S(2)}) async-start(), calls=%async_computation.93 | async-start | bytes 1638400 | tf_op jit(solution)/shard_map/reduce_scatter | solution.py:54
  2066.3 99.9 %reduce-scatter.185.cloned.1.call-start = ((), (), s32[]{:S(2)}) async-start(), calls=%async_computation.158 | async-start | bytes 1310720
  2241.7 78.5 %reduce-scatter.111.cloned.1.call-start = ((), (), s32[]{:S(2)}) async-start(), calls=%async_computation.101 | async-start | bytes 1638400 | tf_op jit(solution)/shard_map/reduce_scatter | solution.py:54
  2477.6 99.2 %reduce-scatter.187.cloned.1.call-start = ((), (), s32[]{:S(2)}) async-start(), calls=%async_computation.159 | async-start | bytes 1310720
  2651.5 78.7 %reduce-scatter.119.cloned.1.call-start = ((), (), s32[]{:S(2)}) async-start(), calls=%async_computation.109 | async-start | bytes 1638400 | tf_op jit(solution)/shard_map/reduce_scatter | solution.py:54
  2885.9 164.3 %reduce-scatter.189.cloned.1.call-start = ((), (), s32[]{:S(2)}) async-start(), calls=%async_computation.160 | async-start | bytes 1310720
  2959.0 101.5 %reduce-scatter.171.cloned.1.call-start = ((), (), s32[]{:S(2)}) async-start(), calls=%async_computation.140 | async-start | bytes 819200 | tf_op jit(solution)/shard_map/reduce_scatter | solution.py:366
  2963.9 96.6 %reduce-scatter.173.cloned.1.call-start = ((), (), s32[]{:S(2)}) async-start(), calls=%async_computation.141 | async-start | bytes 819200 | tf_op jit(solution)/shard_map/reduce_scatter | solution.py:366
  2968.7 92.0 %reduce-scatter.175.cloned.1.call-start = ((), (), s32[]{:S(2)}) async-start(), calls=%async_computation.142 | async-start | bytes 819200 | tf_op jit(solution)/shard_map/reduce_scatter | solution.py:366
  2973.3 111.1 %reduce-scatter.177.cloned.1.call-start = ((), (), s32[]{:S(2)}) async-start(), calls=%async_computation.143 | async-start | bytes 819200 | tf_op jit(solution)/shard_map/reduce_scatter | solution.py:366
  2978.1 132.0 %reduce-scatter.179.cloned.1.call-start = ((), (), s32[]{:S(2)}) async-start(), calls=%async_computation.144 | async-start | bytes 819200 | tf_op jit(solution)/shard_map/reduce_scatter | solution.py:366
  2982.7 156.5 %reduce-scatter.161.cloned.1.call-start = ((), (), s32[]{:S(2)}) async-start(), calls=%async_computation.135 | async-start | bytes 1638400 | tf_op jit(solution)/shard_map/reduce_scatter | solution.py:363
  2987.4 180.8 %reduce-scatter.163.cloned.1.call-start = ((), (), s32[]{:S(2)}) async-start(), calls=%async_computation.136 | async-start | bytes 1638400 | tf_op jit(solution)/shard_map/reduce_scatter | solution.py:363
  2992.1 205.3 %reduce-scatter.165.cloned.1.call-start = ((), (), s32[]{:S(2)}) async-start(), calls=%async_computation.137 | async-start | bytes 1638400 | tf_op jit(solution)/shard_map/reduce_scatter | solution.py:363
  2996.8 229.5 %reduce-scatter.167.cloned.1.call-start = ((), (), s32[]{:S(2)}) async-start(), calls=%async_computation.138 | async-start | bytes 1638400 | tf_op jit(solution)/shard_map/reduce_scatter | solution.py:363
  3001.4 254.0 %reduce-scatter.169.cloned.1.call-start = ((), (), s32[]{:S(2)}) async-start(), calls=%async_computation.139 | async-start | bytes 1638400 | tf_op jit(solution)/shard_map/reduce_scatter | solution.py:363
  3006.5 271.8 %reduce-scatter.151.cloned.1.call-start = ((), (), s32[]{:S(2)}) async-start(), calls=%async_computation.130 | async-start | bytes 409600 | tf_op jit(solution)/shard_map/reduce_scatter | solution.py:360
  3009.4 292.0 %reduce-scatter.153.cloned.1.call-start = ((), (), s32[]{:S(2)}) async-start(), calls=%async_computation.131 | async-start | bytes 409600 | tf_op jit(solution)/shard_map/reduce_scatter | solution.py:360
  3012.4 311.9 %reduce-scatter.155.cloned.1.call-start = ((), (), s32[]{:S(2)}) async-start(), calls=%async_computation.132 | async-start | bytes 409600 | tf_op jit(solution)/shard_map/reduce_scatter | solution.py:360
  3015.3 332.1 %reduce-scatter.157.cloned.1.call-start = ((), (), s32[]{:S(2)}) async-start(), calls=%async_computation.133 | async-start | bytes 409600 | tf_op jit(solution)/shard_map/reduce_scatter | solution.py:360
  3018.2 351.9 %reduce-scatter.159.cloned.1.call-start = ((), (), s32[]{:S(2)}) async-start(), calls=%async_computation.134 | async-start | bytes 409600 | tf_op jit(solution)/shard_map/reduce_scatter | solution.py:360
  3021.2 372.1 %reduce-scatter.131.cloned.1.call-start = ((), (), s32[]{:S(2)}) async-start(), calls=%async_computation.120 | async-start | bytes 409600 | tf_op jit(solution)/shard_map/reduce_scatter | solution.py:354
  3024.0 392.2 %reduce-scatter.133.cloned.1.call-start = ((), (), s32[]{:S(2)}) async-start(), calls=%async_computation.121 | async-start | bytes 409600 | tf_op jit(solution)/shard_map/reduce_scatter | solution.py:354
  3026.8 412.6 %reduce-scatter.135.cloned.1.call-start = ((), (), s32[]{:S(2)}) async-start(), calls=%async_computation.122 | async-start | bytes 409600 | tf_op jit(solution)/shard_map/reduce_scatter | solution.py:354
  3029.7 432.6 %reduce-scatter.137.cloned.1.call-start = ((), (), s32[]{:S(2)}) async-start(), calls=%async_computation.123 | async-start | bytes 409600 | tf_op jit(solution)/shard_map/reduce_scatter | solution.py:354
  3032.5 452.8 %reduce-scatter.139.cloned.1.call-start = ((), (), s32[]{:S(2)}) async-start(), calls=%async_computation.124 | async-start | bytes 409600 | tf_op jit(solution)/shard_map/reduce_scatter | solution.py:354
  3039.3 467.9 %reduce-scatter.141.cloned.1.call-start = ((), (), s32[]{:S(2)}) async-start(), calls=%async_computation.125 | async-start | bytes 204800 | tf_op jit(solution)/shard_map/reduce_scatter | solution.py:357
  3042.0 487.4 %reduce-scatter.143.cloned.1.call-start = ((), (), s32[]{:S(2)}) async-start(), calls=%async_computation.126 | async-start | bytes 204800 | tf_op jit(solution)/shard_map/reduce_scatter | solution.py:357
  3044.6 506.8 %reduce-scatter.145.cloned.1.call-start = ((), (), s32[]{:S(2)}) async-start(), calls=%async_computation.127 | async-start | bytes 204800 | tf_op jit(solution)/shard_map/reduce_scatter | solution.py:357
  3047.3 526.3 %reduce-scatter.147.cloned.1.call-start = ((), (), s32[]{:S(2)}) async-start(), calls=%async_computation.128 | async-start | bytes 204800 | tf_op jit(solution)/shard_map/reduce_scatter | solution.py:357
  3049.9 545.6 %reduce-scatter.149.cloned.1.call-start = ((), (), s32[]{:S(2)}) async-start(), calls=%async_computation.129 | async-start | bytes 204800 | tf_op jit(solution)/shard_map/reduce_scatter | solution.py:357
  3056.7 572.8 %reduce-scatter.125.cloned.1.call-start = ((), (), s32[]{:S(2)}) async-start(), calls=%async_computation.115 | async-start | bytes 1638400 | tf_op jit(solution)/shard_map/reduce_scatter | solution.py:54
  (353 other events, 7346.2 us)
Sparse Core Ops, SparseCore 0:
  12.1 35.3 all-gather.56
  50.3 29.1 all-gather.116
  99.3 29.5 reduce-scatter.70
  214.7 32.7 all-gather.60
  330.2 31.3 all-gather.62
  367.8 30.1 reduce-scatter.76
  494.8 29.5 reduce-scatter.78
  566.4 30.3 reduce-scatter.80
  647.5 29.2 all-gather.124
  727.7 31.3 all-gather.70
  811.7 32.6 all-gather.74
  846.4 31.6 all-gather.112
  880.3 29.1 all-gather.128
  911.5 28.4 all-gather.136
  1069.7 31.3 all-gather.78
  1103.9 30.1 reduce-scatter.126
  1136.3 29.9 reduce-scatter.90
  1313.9 31.3 all-gather.72
  1396.8 29.5 reduce-scatter.94
  1470.0 30.3 reduce-scatter.96
  1583.2 31.3 all-gather.114
  1620.8 30.2 reduce-scatter.128
  1762.1 29.7 reduce-scatter.100
  1830.2 29.2 all-gather.130
  1913.1 31.3 all-gather.90
  1952.7 30.1 reduce-scatter.104
  2066.4 31.3 all-gather.94
  2140.0 26.1 reduce-scatter.184
  2207.7 31.3 all-gather.96
  2290.6 29.5 reduce-scatter.110
  2400.2 31.2 all-gather.100
  2441.0 30.2 reduce-scatter.114
  2584.1 29.7 reduce-scatter.116
  2651.7 29.2 all-gather.134
  2734.5 31.3 all-gather.106
  2774.1 30.1 reduce-scatter.120
  2886.0 31.3 all-gather.110
  2959.2 26.1 reduce-scatter.188
  3011.7 22.4 reduce-scatter.172
  3036.8 22.4 reduce-scatter.174
  3062.0 22.4 reduce-scatter.176
  3087.6 22.4 reduce-scatter.178
  3112.7 26.5 reduce-scatter.160
  3141.7 26.5 reduce-scatter.162
  3170.8 26.5 reduce-scatter.164
  3199.7 26.5 reduce-scatter.166
  3228.9 26.5 reduce-scatter.168
  3598.3 31.2 reduce-scatter.124
  (16 shorter events, 322.9 us)
Sparse Core Ops, SparseCore 1:
  101.7 16.3 all-gather.118
  133.3 31.2 all-gather.58
  170.8 30.3 reduce-scatter.72
  250.2 29.0 all-gather.120
  296.1 29.5 reduce-scatter.74
  413.6 32.4 all-gather.64
  448.8 29.1 all-gather.122
  528.9 31.2 all-gather.66
  612.2 32.5 all-gather.68
  693.6 29.5 reduce-scatter.82
  764.9 30.2 reduce-scatter.84
  961.0 29.5 reduce-scatter.86
  994.8 31.1 all-gather.76
  1034.1 30.3 reduce-scatter.88
  1173.1 31.2 all-gather.80
  1246.4 26.2 reduce-scatter.180
  1279.9 29.8 reduce-scatter.92
  1347.9 29.0 all-gather.126
  1430.5 31.2 all-gather.82
  1506.3 31.1 all-gather.84
  1547.0 30.3 reduce-scatter.98
  1655.2 31.2 all-gather.86
  1728.6 26.2 reduce-scatter.182
  1796.3 31.2 all-gather.88
  1879.3 29.5 reduce-scatter.102
  1988.9 31.1 all-gather.92
  2029.6 30.3 reduce-scatter.106
  2173.4 29.8 reduce-scatter.108
  2241.8 29.1 all-gather.132
  2324.4 31.2 all-gather.98
  2363.8 30.3 reduce-scatter.112
  2477.7 31.2 all-gather.102
  2550.5 26.2 reduce-scatter.186
  2617.7 31.2 all-gather.104
  2700.7 29.5 reduce-scatter.118
  2809.7 31.1 all-gather.108
  2850.4 30.3 reduce-scatter.122
where the time goes:
time: 3720 us; the launch traced here: 3710 us
  waiting for transfers between devices  2650 us (71%)
  matrix products  376 us (10%)
  other arithmetic  314 us (8%)
  local copies, waits for them, and re-layouts  232 us (6%)
  blocking collectives  87.4 us (2%)
    all_gather x30, waiting for transfers between devices, collect(): return lax.all_gather(rows, 'tensor', axis=0, tiled=True)  908 us
    reduce_scatter x30, waiting for transfers between devices, spread_total_sum(): lax.psum_scatter(total.astype(jnp.bfloat16), 'tensor', scatter_dimension=...  882 us
    all_gather x10, waiting for transfers between devices, layer_forward(): keyval = lax.all_gather(keyval_part, 'tensor', axis=2, tiled=True)  219 us
    reduce_scatter x5, waiting for transfers between devices, body(): lax.psum_scatter(grad_weights[3].astype(jnp.bfloat16), 'dp', scatter_dime...  143 us
    unnamed x337, local copies, waits for them, and re-layouts  114 us
    reduce_scatter x5, waiting for transfers between devices, body(): lax.psum_scatter(grad_weights[0].astype(jnp.bfloat16), 'dp', scatter_dime...  113 us
    reduce_scatter x5, waiting for transfers between devices, body(): lax.psum_scatter(grad_weights[2].astype(jnp.bfloat16), 'dp', scatter_dime...  112 us
    reduce_scatter x5, waiting for transfers between devices, body(): lax.psum_scatter(grad_weights[1].astype(jnp.bfloat16), 'dp', scatter_dime...  109 us
  transfers between devices with their start and end apart: 109, of which 100 were waited for; matrix products, arithmetic and copies ran while one was open for 6% of the time, Pallas kernels for 0%

commit v1 on v0

v1 whole, which is shorter than its diff:
```python
import jax
import jax.numpy as jnp
from jax import lax
from jax.sharding import PartitionSpec as P

HD = 256
WIN = 512

BASES = (10000.0, 1000000.0)
EPS = 1e-06
EVERY = ("tensor", "dp", "section")
BF = jnp.bfloat16
F32 = jnp.float32


def dots(pattern, left, right):
    return jnp.einsum(pattern, left, right, preferred_element_type=F32)


def swap(array):
    return lax.ppermute(array, "section", [(0, 1), (1, 0)])


def rms_scale(rows, gain):
    return rows * lax.rsqrt(jnp.mean(rows * rows, axis=-1, keepdims=True) + EPS) * gain


def rotary_tables(places, base):
    freqs = jnp.exp(-jnp.log(jnp.float32(base)) * jnp.arange(HD // 2, dtype=F32) * (2.0 / HD))
    angles = places.astype(F32)[:, None] * freqs
    return jnp.cos(angles), jnp.sin(angles)


def rotated(values, gain, tables):
    cosine, sine = tables
    values = rms_scale(values, gain)
    front, back = values[..., : HD // 2], values[..., HD // 2 :]
    return jnp.concatenate([front * cosine - back * sine, back * cosine + front * sine], axis=-1)


def gated(gate, up):
    return jax.nn.gelu(gate, approximate=True) * up


def layer_forward(rows, attn_weights, ff_weights, gains, qk_gain, tables, mask):
    w_query, w_keyval, w_out = attn_weights
    w_gateup, w_down = ff_weights
    heads = w_query.shape[0]
    length = rows.shape[0]
    normed = rms_scale(rows, gains[0]).astype(BF)
    keyval = dots("ld,tdc->ltc", normed, w_keyval).reshape(length, 2 * HD).astype(BF)
    keys_raw = keyval[:, :HD].astype(F32)
    own = jnp.concatenate([rotated(keys_raw, qk_gain[1], tables).astype(BF), keyval[:, HD:]], axis=1)
    both = jnp.concatenate([own, swap(own)], axis=0)
    keys, values = both[:, :HD], both[:, HD:]
    query_raw = dots("ld,tdc->tlc", normed, w_query)
    query = rotated(query_raw, qk_gain[0], tables).astype(BF)
    scores = dots("hqd,kd->hqk", query, keys) * (HD ** -0.5)
    scores = jnp.where(mask[None], scores, -1e30)
    peak = jnp.max(scores, axis=-1, keepdims=True)
    weights = jnp.exp(scores - peak)
    probs = (weights / jnp.sum(weights, axis=-1, keepdims=True)).astype(BF)
    mixed = dots("hqk,kd->hqd", probs, values).astype(BF)
    branch = dots("hqe,hde->qd", mixed, w_out)
    middle = rows + rms_scale(branch, gains[1])
    normed_ff = rms_scale(middle, gains[2]).astype(BF)
    gateup = dots("ld,tdc->tlc", normed_ff, w_gateup)
    half = gateup.shape[-1] // 2
    hidden = gated(gateup[..., :half], gateup[..., half:]).astype(BF)
    branch_ff = dots("tlf,tdf->ld", hidden, w_down)
    output = middle + rms_scale(branch_ff, gains[3])
    kept = (rows, normed, keys_raw, query_raw, query, keys, values, probs, mixed, branch, middle,
            normed_ff, gateup, hidden, branch_ff)
    return output, kept


def layer_backward(kept, attn_weights, ff_weights, gains, qk_gain, tables, grad_output):
    (rows, normed, keys_raw, query_raw, query, keys, values, probs, mixed, branch, middle,
     normed_ff, gateup, hidden, branch_ff) = kept
    w_query, w_keyval, w_out = attn_weights
    w_gateup, w_down = ff_weights
    length = rows.shape[0]
    parts = w_query.shape[0]
    _, pull = jax.vjp(rms_scale, branch_ff, gains[3])
    d_branch_ff, dg3 = pull(grad_output)
    d_branch_ff = d_branch_ff.astype(BF)
    d_hidden = dots("ld,tdf->tlf", d_branch_ff, w_down)
    g_down = dots("ld,tlf->tdf", d_branch_ff, hidden).astype(BF)
    half = gateup.shape[-1] // 2
    _, pull = jax.vjp(gated, gateup[..., :half], gateup[..., half:])
    d_gate, d_up = pull(d_hidden)
    d_gateup = jnp.concatenate([d_gate.astype(BF), d_up.astype(BF)], axis=-1)
    g_gateup = dots("ld,tlc->tdc", normed_ff, d_gateup).astype(BF)
    ff_share = scatter_total((g_gateup, g_down))
    d_normed_ff = dots("tlc,tdc->ld", d_gateup, w_gateup)
    _, pull = jax.vjp(rms_scale, middle, gains[2])
    d_middle, dg2 = pull(d_normed_ff)
    d_middle = d_middle + grad_output
    _, pull = jax.vjp(rms_scale, branch, gains[1])
    d_branch, dg1 = pull(d_middle)
    d_branch = d_branch.astype(BF)
    d_mixed = dots("qd,hde->hqe", d_branch, w_out).astype(BF)
    g_out = dots("qd,hqe->hde", d_branch, mixed).astype(BF)
    d_probs = dots("hqd,kd->hqk", d_mixed, values)
    wide = probs.astype(F32)
    inner = jnp.sum(wide * d_probs, axis=-1, keepdims=True)
    d_scores = (wide * (d_probs - inner)).astype(BF)
    scale = HD ** -0.5
    d_keys = dots("hqk,hqd->kd", d_scores, query) * scale
    d_values = dots("hqk,hqd->kd", probs, d_mixed)
    d_both = jnp.concatenate([d_keys, d_values], axis=1)
    arrived = swap(d_both[length:].astype(BF))
    d_query = dots("hqk,kd->hqd", d_scores, keys) * scale
    _, pull = jax.vjp(lambda raw, gain: rotated(raw, gain, tables), query_raw, qk_gain[0])
    d_query_raw, dgq = pull(d_query)
    d_query_raw = d_query_raw.astype(BF)
    d_both = d_both[:length] + arrived.astype(F32)
    _, pull = jax.vjp(lambda raw, gain: rotated(raw, gain, tables), keys_raw, qk_gain[1])
    d_keys_raw, dgk = pull(d_both[:, :HD])
    d_keyval = jnp.concatenate([d_keys_raw, d_both[:, HD:]], axis=1).astype(BF)
    d_keyval = d_keyval.reshape(length, parts, 2 * HD // parts)
    g_query = dots("ld,tlc->tdc", normed, d_query_raw).astype(BF)
    g_keyval = dots("ld,ltc->tdc", normed, d_keyval).astype(BF)
    attn_share = scatter_total((g_query, g_keyval, g_out))
    d_normed = dots("tlc,tdc->ld", d_query_raw, w_query) + dots("ltc,tdc->ld", d_keyval, w_keyval)
    _, pull = jax.vjp(rms_scale, rows, gains[0])
    d_rows, dg0 = pull(d_normed)
    d_rows = d_rows + d_middle
    small = jnp.concatenate([dg0, dg1, dg2, dg3, dgq, dgk])
    return d_rows, attn_share, ff_share, small


def gathered(shard, widths):
    tensor = lax.axis_size("tensor")
    whole = lax.all_gather(shard, EVERY, axis=0, tiled=True)
    whole = whole.reshape(tensor, whole.shape[0] // tensor, whole.shape[1])
    pieces, at = [], 0
    for width in widths:
        pieces.append(whole[:, :, at : at + width])
        at += width
    return tuple(pieces)


def scatter_total(grads):
    packed = jnp.concatenate(grads, axis=2)
    packed = packed.reshape(packed.shape[0] * packed.shape[1], packed.shape[2])
    return lax.psum_scatter(packed, EVERY, scatter_dimension=0, tiled=True)


def body(
    boundary, positions, w_query, w_keyval, w_out, w_gateup, down_weight, norm_gains, qk_gains
):
    section = lax.axis_index("section")
    first = section == 0
    tensor = lax.axis_size("tensor")
    local = boundary[0][:, :, 0]
    micro, span, width = local.shape
    part = span // 2

    attn = jnp.concatenate([w_query[0], w_keyval[0], w_out[0].T], axis=1)
    ff_in = w_gateup[0].reshape(w_gateup.shape[1], -1)
    ff = jnp.concatenate([ff_in, down_weight[0].T], axis=1)
    attn_widths = (w_query.shape[2], w_keyval.shape[2], w_out.shape[1])
    ff_widths = (ff_in.shape[1], down_weight.shape[1])
    packed = jnp.concatenate([attn, ff], axis=1)
    rows_half = packed.shape[0] // 2
    top, bottom = packed[:rows_half], packed[rows_half:]
    mine = jnp.where(first, top, bottom)
    other = swap(jnp.where(first, bottom, top))
    layers = (jnp.where(first, mine, other), jnp.where(first, other, mine))
    cut = attn.shape[1]
    attn_w = [None, None]
    ff_w = [None, None]
    for index in range(2):
        attn_w[index] = gathered(layers[index][:, :cut], attn_widths)
        ff_w[index] = gathered(layers[index][:, cut:], ff_widths)

    gains = lax.all_gather(
        jnp.concatenate([norm_gains[0].reshape(-1), qk_gains[0].reshape(-1)]), "section", axis=0
    )
    split = norm_gains.shape[1] * norm_gains.shape[2]
    norm_all = gains[:, :split].reshape(2, norm_gains.shape[1], norm_gains.shape[2])
    qk_all = gains[:, split:].reshape(2, 2, HD)

    sent = local.reshape(micro, 2, part, width).transpose(1, 0, 2, 3)
    sent = sent.reshape(2 * micro, part, width)
    came = lax.all_to_all(sent, ("section", "tensor"), 0, 0, tiled=True)
    rows = came[:micro].reshape(micro * part, width).astype(F32)
    cotangent = came[micro:].reshape(micro * part, width).astype(F32)

    places = lax.dynamic_index_in_dim(
        positions[:, :, 0], lax.axis_index("tensor"), 0, keepdims=False
    )
    documents = jnp.cumsum((places == 0).astype(jnp.int32))

    def halves(values):
        values = values.reshape(micro, 2, part)
        even, odd = values[:, 0].reshape(-1), values[:, 1].reshape(-1)
        return jnp.where(first, even, odd), jnp.where(first, odd, even)

    own_pos, other_pos = halves(places)
    own_doc, other_doc = halves(documents)
    key_pos = jnp.concatenate([own_pos, other_pos])
    key_doc = jnp.concatenate([own_doc, other_doc])
    gap = own_pos[:, None] - key_pos[None, :]
    causal = (own_doc[:, None] == key_doc[None, :]) & (gap >= 0)
    masks = (causal & (gap < WIN), causal)
    tables = tuple(rotary_tables(own_pos, base) for base in BASES)

    kept = [None, None]
    for index in range(2):
        output, kept[index] = layer_forward(
            rows, attn_w[index], ff_w[index], norm_all[index], qk_all[index], tables[index],
            masks[index],
        )
        rows = output.astype(BF).astype(F32)
    grad = cotangent
    shares = [None, None]
    smalls = [None, None]
    for index in (1, 0):
        grad_rows, attn_share, ff_share, smalls[index] = layer_backward(
            kept[index], attn_w[index], ff_w[index], norm_all[index], qk_all[index],
            tables[index], grad,
        )
        shares[index] = jnp.concatenate([attn_share, ff_share], axis=1)
        grad = grad_rows.astype(BF).astype(F32)

    back = jnp.stack([grad_rows.astype(BF), output.astype(BF)]).reshape(2 * micro, part, width)
    back = lax.all_to_all(back, ("section", "tensor"), 0, 0, tiled=True)
    ends = back.reshape(2, micro, part, width).transpose(1, 0, 2, 3).reshape(micro, span, width)
    ends = ends.astype(F32)[None, :, :, None]

    passed = swap(jnp.where(first, shares[1], shares[0]))
    stayed = jnp.where(first, shares[0], shares[1])
    grads = jnp.concatenate(
        [jnp.where(first, stayed, passed), jnp.where(first, passed, stayed)], axis=0
    ).astype(F32)
    found, at = [], 0
    for size in attn_widths + ff_widths:
        found.append(grads[:, at : at + size])
        at += size
    small = lax.psum(jnp.stack(smalls), ("section", "dp", "tensor"))
    small = lax.dynamic_index_in_dim(small, section, 0, keepdims=False)
    return (
        ends,
        found[0][None],
        found[1][None],
        found[2].T[None],
        found[3].reshape(w_gateup.shape),
        found[4].T[None],
        small[:split].reshape(norm_gains.shape),
        small[split:].reshape(qk_gains.shape),
    )


def solution(mesh):
    in_specs = (
        P("section", None, "tensor", "dp", None),
        P(None, None, "dp"),
        P("section", "dp", "tensor"),
        P("section", "dp", "tensor"),
        P("section", "tensor", "dp"),
        P("section", "dp", None, "tensor"),
        P("section", "tensor", "dp"),
        P("section", None, None),
        P("section", None, None),
    )
    out_specs = (
        P("section", None, "tensor", "dp", None),
        P("section", "dp", "tensor"),
        P("section", "dp", "tensor"),
        P("section", "tensor", "dp"),
        P("section", "dp", None, "tensor"),
        P("section", "tensor", "dp"),
        P("section", None, None),
        P("section", None, None),
    )
    return jax.shard_map(body, mesh=mesh, in_specs=in_specs, out_specs=out_specs, check_vma=False)
```

time: 3720 us -> 1010 us (0.27)
  waiting for transfers between devices: 2650 us -> 623 us
  matrix products: 376 us -> 128 us
  other arithmetic: 314 us -> 82.8 us
  local copies, waits for them, and re-layouts: 232 us -> 84.6 us
  blocking collectives: 87.4 us -> 48.3 us
    reduce_scatter x55 -> x4, waiting for transfers between devices: 1410 us -> 416 us  [scatter_total(): return lax.psum_scatter(packed, EVERY, scatter_dimension=0, tiled=True)]
    all_gather x41 -> x4, waiting for transfers between devices: 1130 us -> 147 us  [gathered(): whole = lax.all_gather(shard, EVERY, axis=0, tiled=True)]
    dot_general x190 -> x41, matrix products: 376 us -> 128 us  [dots(): return jnp.einsum(pattern, left, right, preferred_element_type=F32)]
    reduce_sum x95 -> x14, other arithmetic: 110 us -> 8.28 us  [the longest x8 5.66 us: rms_scale(): rows * lax.rsqrt(jnp.mean(rows * rows, axis=-1, keepdims=True) + EPS) * gain]
    while x286 -> x0, local copies, waits for them, and re-layouts: 90.7 us -> none
    unnamed x106 -> x8, waiting for transfers between devices: 83.9 us -> 0.16 us
    unnamed x337 -> x282, local copies, waits for them, and re-layouts: 114 us -> 36.6 us
    another operation x82 -> x13, other arithmetic: 74.7 us -> 5.37 us
  transfers between devices with their start and end apart: 109 -> 16, of which waited for: 100 -> 13; matrix products, arithmetic and copies ran while one was open for 6% -> 19% of each run, Pallas kernels for 0% -> 0%
where the time goes in v1:
time: 1010 us
  waiting for transfers between devices  623 us (62%)
  matrix products  128 us (13%)
  local copies, waits for them, and re-layouts  84.6 us (8%)
  other arithmetic  82.8 us (8%)
  blocking collectives  48.3 us (5%)
  starting transfers between devices  21.6 us (2%)
  between operations  16.5 us (2%)
    reduce_scatter x4, waiting for transfers between devices, scatter_total(): return lax.psum_scatter(packed, EVERY, scatter_dimension=0, tiled=True)  416 us
    all_gather x4, waiting for transfers between devices, gathered(): whole = lax.all_gather(shard, EVERY, axis=0, tiled=True)  147 us
    dot_general x41, matrix products, dots(): return jnp.einsum(pattern, left, right, preferred_element_type=F32)  128 us
    ppermute x6, waiting for transfers between devices, swap(): return lax.ppermute(array, 'section', [(0, 1), (1, 0)])  41 us
    psum x1, blocking collectives, body(): small = lax.psum(jnp.stack(smalls), ('section', 'dp', 'tensor'))  40.3 us
    unnamed x282, local copies, waits for them, and re-layouts  36.6 us
    concatenate x4, local copies, waits for them, and re-layouts, scatter_total(): packed = jnp.concatenate(grads, axis=2)  28.7 us
  transfers between devices with their start and end apart: 16, of which 13 were waited for; matrix products, arithmetic and copies ran while one was open for 19% of the time, Pallas kernels for 0%

profile of v1, /device:TPU:0, one launch (start us, length us, event | category | flops | bytes accessed | tf_op | source)
XLA Modules:
  0.0 1005.6 jit_solution(125647902550046203)
XLA Ops:
  11.8 3.0 collective-permute-start
  14.8 8.1 collective-permute-done
  26.5 6.1 all-to-all-start
  32.7 8.1 all-gather
  47.2 18.9 %all-to-all-done = bf16[8,128,640]{2,1,0:T(8,128)(2,1)S(1)} async-done(((bf16[8,128,640]{2,1,0:T(8,128)(2,1)}), bf16[8,128,640]{2,1,0:T(8,128)(2,1)S(1)}, u32[]{:S(2)}, u32[]{:S(2)}) %all-to-all-start) | async-done | bytes 1310752 | tf_op jit(solution)/shard_map/all_to_all | solution.py:187
  67.9 29.6 %all-gather.6.cloned.1.call-done = bf16[2560,640]{1,0:T(8,128)(2,1)} async-done(((bf16[80,640]{1,0:T(8,128)(2,1)}), bf16[2560,640]{1,0:T(8,128)(2,1)}) %all-gather.6.cloned.1.call-update) | async-done | bytes 3276816 | tf_op jit(solution)/shard_map/all_gather | solution.py:135
  106.1 53.1 %all-gather.10.cloned.1.call-done = bf16[2560,640]{1,0:T(8,128)(2,1)} async-done(((bf16[80,640]{1,0:T(8,128)(2,1)}), bf16[2560,640]{1,0:T(8,128)(2,1)}) %all-gather.10.cloned.1.call-update) | async-done | bytes 3276816 | tf_op jit(solution)/shard_map/all_gather | solution.py:135
  167.2 4.6 fusion.133
  171.8 9.8 fusion.232
  186.8 2.9 multiply_reduce_fusion.15
  190.8 46.3 %all-gather.8.cloned.1.call-done = bf16[2560,1536]{1,0:T(8,128)(2,1)} async-done(((bf16[80,1536]{1,0:T(8,128)(2,1)}), bf16[2560,1536]{1,0:T(8,128)(2,1)}) %all-gather.8.cloned.1.call-update) | async-done | bytes 7864336 | tf_op jit(solution)/shard_map/all_gather | solution.py:135
  237.1 6.1 fusion.38
  246.4 4.5 multiply_reduce_fusion.13
  259.4 12.2 %collective-permute-done.2 = bf16[512,512]{0,1:T(8,128)(2,1)S(1)} collective-permute-done((bf16[512,512]{0,1:T(8,128)(2,1)S(1)}, bf16[512,512]{0,1:T(8,128)(2,1)S(1)}, u32[]{:S(2)}, u32[]{:S(2)}) %collective-permute-start.2) | collective-permute-done | bytes 524320 | tf_op jit(solution)/shard_map/ppermute | solution.py:21
  271.7 4.6 fusion.132
  276.3 9.9 fusion.233
  297.3 18.3 %all-gather.12.cloned.1.call-done = bf16[2560,1536]{1,0:T(8,128)(2,1)} async-done(((bf16[80,1536]{1,0:T(8,128)(2,1)}), bf16[2560,1536]{1,0:T(8,128)(2,1)}) %all-gather.12.cloned.1.call-update) | async-done | bytes 7864336 | tf_op jit(solution)/shard_map/all_gather | solution.py:135
  315.6 6.1 fusion.41
  329.6 4.8 fusion.29
  334.4 3.7 multiply_reduce_fusion.2
  339.2 3.0 fusion.84
  345.0 2.9 fusion.5
  347.9 3.7 convolution_multiply_fusion.1
  360.1 3.4 convolution_bitcast_fusion.3
  365.7 7.0 collective-permute-done.3
  381.5 8.4 fusion.22
  390.0 3.6 multiply_reduce_fusion.4
  395.8 3.5 fusion.85
  399.6 3.6 copy.201
  404.8 3.6 fusion.2
  408.3 4.4 fusion.3
  427.2 13.6 %collective-permute-done.4 = bf16[512,512]{0,1:T(8,128)(2,1)S(1)} collective-permute-done((bf16[512,512]{0,1:T(8,128)(2,1)S(1)}, bf16[512,512]{0,1:T(8,128)(2,1)S(1)}, u32[]{:S(2)}, u32[]{:S(2)}) %collective-permute-start.4) | collective-permute-done | bytes 524320 | tf_op jit(solution)/shard_map/ppermute | solution.py:21
  446.2 3.6 copy.197
  451.4 4.5 convert_bitcast_fusion.2
  455.9 6.8 convert_bitcast_fusion
  462.7 7.1 pad_maximum_fusion.1
  469.8 10.7 %copy.202 = bf16[4,640,1536]{2,1,0:T(8,128)(2,1)} copy(bf16[4,640,1536]{1,2,0:T(8,128)(2,1)} %pad_maximum_fusion.1) | data formatting | bytes 15728640 | tf_op jit(solution)/shard_map/concatenate | solution.py:145
  482.1 4.5 convert_bitcast_fusion.3
  486.6 6.6 convert_bitcast_fusion.1
  493.2 7.1 pad_maximum_fusion
  500.3 10.7 %copy.198 = bf16[4,640,1536]{2,1,0:T(8,128)(2,1)} copy(bf16[4,640,1536]{1,2,0:T(8,128)(2,1)} %pad_maximum_fusion) | data formatting | bytes 15728640 | tf_op jit(solution)/shard_map/concatenate | solution.py:145
  519.2 4.7 all-to-all-start.1
  523.9 25.7 %reduce-scatter.9.cloned.1.call-done = bf16[80,640]{1,0:T(8,128)(2,1)} async-done(((bf16[2560,640]{1,0:T(8,128)(2,1)}), bf16[80,640]{1,0:T(8,128)(2,1)}) %reduce-scatter.9.cloned.1.call-update) | async-done | bytes 102416 | tf_op jit(solution)/shard_map/reduce_scatter | solution.py:147
  550.5 140.1 %reduce-scatter.5.cloned.1.call-done = bf16[80,640]{1,0:T(8,128)(2,1)} async-done(((bf16[2560,640]{1,0:T(8,128)(2,1)}), bf16[80,640]{1,0:T(8,128)(2,1)}) %reduce-scatter.5.cloned.1.call-update) | async-done | bytes 102416 | tf_op jit(solution)/shard_map/reduce_scatter | solution.py:147
  691.4 123.1 %reduce-scatter.11.cloned.1.call-done = bf16[80,1536]{1,0:T(8,128)(2,1)} async-done(((bf16[2560,1536]{1,0:T(8,128)(2,1)}), bf16[80,1536]{1,0:T(8,128)(2,1)}) %reduce-scatter.11.cloned.1.call-update) | async-done | bytes 245776 | tf_op jit(solution)/shard_map/reduce_scatter | solution.py:147
  815.5 127.2 %reduce-scatter.7.cloned.1.call-done = bf16[80,1536]{1,0:T(8,128)(2,1)} async-done(((bf16[2560,1536]{1,0:T(8,128)(2,1)}), bf16[80,1536]{1,0:T(8,128)(2,1)}) %reduce-scatter.7.cloned.1.call-update) | async-done | bytes 245776 | tf_op jit(solution)/shard_map/reduce_scatter | solution.py:147
  946.0 40.3 %psum.7 = f32[2,3072]{1,0:T(2,128)S(1)} all-reduce(f32[2,3072]{1,0:T(2,128)S(1)} %pad_maximum_fusion.34), channel_id=1, replica_groups=mesh['section'=2,'dp'=4,'tensor'=4] {'section','dp','tensor'}, use_global_device_ids=true, to_apply=%region_48.49 | all-reduce | flops 6144 | bytes 49152 | tf_op jit(solution)/shard_map/psum | solution.py:242
  990.2 3.6 reshape.687
  (465 shorter events, 141.8 us)
Async XLA Ops:
  7.2 90.4 %all-gather.6.cloned.1.call-start = ((), (), s32[]{:S(2)}) async-start(), calls=%async_computation.6 | async-start | bytes 3379200 | tf_op jit(solution)/shard_map/all_gather | solution.py:135
  11.8 13.5 %copy-start.62 = (bf16[1,4,256,1,640]{4,2,3,1,0:T(8,128)(2,1)S(1)}, bf16[1,4,256,1,640]{4,2,3,1,0:T(8,128)(2,1)}, u32[]{:S(2)}) copy-start(bf16[1,4,256,1,640]{4,2,3,1,0:T(8,128)(2,1)} %param.9) | copy-start | bytes 3932164
  11.8 11.2 %collective-permute-start = (bf16[80,2176]{1,0:T(8,128)(2,1)S(1)}, bf16[80,2176]{1,0:T(8,128)(2,1)S(1)}, u32[]{:S(2)}, u32[]{:S(2)}) collective-permute-start(bf16[80,2176]{1,0:T(8,128)(2,1)S(1)} %broadcast_select_fusion.6), channel_id=1, source_target_pairs={{0,16},{16,0},{1,17},{17,1},{2,18},{18,2},{3,19},{19,3},{4,20},{20... | collective-permute-start | bytes 1044488 | tf_op jit(solution)/shard_map/ppermute | solution.py:21
  23.8 135.4 %all-gather.10.cloned.1.call-start = ((), (), s32[]{:S(2)}) async-start(), calls=%async_computation.8 | async-start | bytes 3379200 | tf_op jit(solution)/shard_map/all_gather | solution.py:135
  24.5 212.6 %all-gather.8.cloned.1.call-start = ((), (), s32[]{:S(2)}) async-start(), calls=%async_computation.7 | async-start | bytes 8110080 | tf_op jit(solution)/shard_map/all_gather | solution.py:135
  25.3 7.3 copy-start.112
  25.3 7.3 copy-start.106
  26.5 39.7 %all-to-all-start = ((bf16[8,128,640]{2,1,0:T(8,128)(2,1)}), bf16[8,128,640]{2,1,0:T(8,128)(2,1)S(1)}, u32[]{:S(2)}, u32[]{:S(2)}) async-start(bf16[8,128,640]{2,1,0:T(8,128)(2,1)} %bitcast.16), calls=%async_computation | async-start | bytes 2621440 | tf_op jit(solution)/shard_map/all_to_all | solution.py:187
  32.6 283.1 %all-gather.12.cloned.1.call-start = ((), (), s32[]{:S(2)}) async-start(), calls=%async_computation.9 | async-start | bytes 8110080 | tf_op jit(solution)/shard_map/all_gather | solution.py:135
  43.9 23.8 %copy-start.83 = (f32[640]{0:T(1024)}, f32[640]{0:T(1024)S(1)}, u32[]{:S(2)}) copy-start(f32[640]{0:T(1024)S(1)} %get-tuple-element.39) | copy-start | bytes 7684
  44.5 57.1 %copy-start.96 = (f32[1,256]{1,0:T(1,128)}, f32[1,256]{1,0:T(1,128)S(1)}, u32[]{:S(2)}) copy-start(f32[1,256]{1,0:T(1,128)S(1)} %get-tuple-element.81) | copy-start | bytes 3076
  47.2 502.4 %reduce-scatter.9.cloned.1.call-start = ((), (), s32[]{:S(2)}) async-start(), calls=%async_computation.12 | async-start | bytes 3379200 | tf_op jit(solution)/shard_map/reduce_scatter | solution.py:147
  66.2 123.6 %copy-start.6 = (bf16[8,128,640]{2,1,0:T(8,128)(2,1)}, bf16[8,128,640]{2,1,0:T(8,128)(2,1)S(1)}, u32[]{:S(2)}) copy-start(bf16[8,128,640]{2,1,0:T(8,128)(2,1)S(1)} %all-to-all-done) | copy-start | bytes 3932164
  66.4 32.3 %copy-start.88 = (f32[4,128]{1,0:T(4,128)}, f32[4,128]{1,0:T(4,128)S(1)}, u32[]{:S(2)}) copy-start(f32[4,128]{1,0:T(4,128)S(1)} %fusion.110) | copy-start | bytes 6148
  66.4 32.3 %copy-start.92 = (f32[512]{0:T(512)}, f32[512]{0:T(512)S(1)}, u32[]{:S(2)}) copy-start(f32[512]{0:T(512)S(1)} %bitcast_rsqrt_fusion) | copy-start | bytes 6148
  67.7 93.7 %copy-start.40 = (bf16[512,640]{1,0:T(8,128)(2,1)}, bf16[512,640]{1,0:T(8,128)(2,1)S(1)}, u32[]{:S(2)}) copy-start(bf16[512,640]{1,0:T(8,128)(2,1)S(1)} %fusion.108) | copy-start | bytes 1966084
  103.8 55.4 %copy-start.65 = (bf16[512,128]{0,1:T(8,128)(2,1)}, bf16[512,128]{0,1:T(8,128)(2,1)S(1)}, u32[]{:S(2)}) copy-start(bf16[512,128]{0,1:T(8,128)(2,1)S(1)} %get-tuple-element.78) | copy-start | bytes 393220
  103.8 61.3 %copy-start.42 = (f32[512,128]{0,1:T(8,128)}, f32[512,128]{0,1:T(8,128)S(1)}, u32[]{:S(2)}) copy-start(f32[512,128]{0,1:T(8,128)S(1)} %get-tuple-element.91) | copy-start | bytes 786436
  103.8 61.3 %copy-start.44 = (f32[512,128]{0,1:T(8,128)}, f32[512,128]{0,1:T(8,128)S(1)}, u32[]{:S(2)}) copy-start(f32[512,128]{0,1:T(8,128)S(1)} %get-tuple-element.92) | copy-start | bytes 786436
  104.7 60.9 %collective-permute-start.1 = (bf16[512,512]{0,1:T(8,128)(2,1)}, bf16[512,512]{0,1:T(8,128)(2,1)}, u32[]{:S(2)}, u32[]{:S(2)}) collective-permute-start(bf16[512,512]{0,1:T(8,128)(2,1)} %pad_maximum_fusion.25), channel_id=1, source_target_pairs={{0,16},{16,0},{1,17},{17,1},{2,18},{18,2},{3,19},{19,3},{4,20},{20... | collective-permute-start | bytes 1572872 | tf_op jit(solution)/shard_map/ppermute | solution.py:21
  165.5 6.2 copy-start.50
  165.5 6.2 copy-start.52
  167.2 15.6 %copy-start.29 = (bf16[1024,512]{0,1:T(8,128)(2,1)}, bf16[1024,512]{0,1:T(8,128)(2,1)S(1)}, u32[]{:S(2)}) copy-start(bf16[1024,512]{0,1:T(8,128)(2,1)S(1)} %pad_maximum_fusion.18) | copy-start | bytes 3145732
  189.7 47.4 %copy-start.100 = (f32[640]{0:T(1024)S(1)}, f32[640]{0:T(1024)}, u32[]{:S(2)}) copy-start(f32[640]{0:T(1024)} %get-tuple-element.37) | copy-start | bytes 7684
  190.8 202.9 %copy-start.10 = (f32[512,640]{1,0:T(8,128)}, f32[512,640]{1,0:T(8,128)S(1)}, u32[]{:S(2)}) copy-start(f32[512,640]{1,0:T(8,128)S(1)} %get-tuple-element.48) | copy-start | bytes 3932164
  251.3 43.5 %copy-start.26 = (bf16[512,640]{1,0:T(8,128)(2,1)}, bf16[512,640]{1,0:T(8,128)(2,1)S(1)}, u32[]{:S(2)}) copy-start(bf16[512,640]{1,0:T(8,128)(2,1)S(1)} %get-tuple-element.46) | copy-start | bytes 1966084
  254.7 16.9 %collective-permute-start.2 = (bf16[512,512]{0,1:T(8,128)(2,1)S(1)}, bf16[512,512]{0,1:T(8,128)(2,1)S(1)}, u32[]{:S(2)}, u32[]{:S(2)}) collective-permute-start(bf16[512,512]{0,1:T(8,128)(2,1)S(1)} %pad_maximum_fusion.26), channel_id=1, source_target_pairs={{0,16},{16,0},{1,17},{17,1},{2,18},{18,2},{3,19},{19,3},{4,20},{20... | collective-permute-start | bytes 1572872 | tf_op jit(solution)/shard_map/ppermute | solution.py:21
  259.3 16.9 %copy-start.54 = (bf16[4,512,128]{1,2,0:T(8,128)(2,1)}, bf16[4,512,128]{1,2,0:T(8,128)(2,1)S(1)}, u32[]{:S(2)}) copy-start(bf16[4,512,128]{1,2,0:T(8,128)(2,1)S(1)} %get-tuple-element.59) | copy-start | bytes 1572868
  259.4 16.9 %copy-start.56 = (bf16[4,512,128]{1,2,0:T(8,128)(2,1)}, bf16[4,512,128]{1,2,0:T(8,128)(2,1)S(1)}, u32[]{:S(2)}) copy-start(bf16[4,512,128]{1,2,0:T(8,128)(2,1)S(1)} %get-tuple-element.60) | copy-start | bytes 1572868
  271.7 15.6 %copy-start.31 = (bf16[1024,512]{0,1:T(8,128)(2,1)}, bf16[1024,512]{0,1:T(8,128)(2,1)S(1)}, u32[]{:S(2)}) copy-start(bf16[1024,512]{0,1:T(8,128)(2,1)S(1)} %pad_maximum_fusion.20) | copy-start | bytes 3145732
  294.8 20.8 %copy-start.101 = (f32[640]{0:T(1024)S(1)}, f32[640]{0:T(1024)}, u32[]{:S(2)}) copy-start(f32[640]{0:T(1024)} %get-tuple-element.33) | copy-start | bytes 7684
  358.6 14.2 %collective-permute-start.3 = (bf16[512,512]{0,1:T(8,128)(2,1)S(1)}, bf16[512,512]{0,1:T(8,128)(2,1)S(1)}, u32[]{:S(2)}, u32[]{:S(2)}) collective-permute-start(bf16[512,512]{0,1:T(8,128)(2,1)S(1)} %fusion.131), channel_id=1, source_target_pairs={{0,16},{16,0},{1,17},{17,1},{2,18},{18,2},{3,19},{19,3},{4,20},{20... | collective-permute-start | bytes 1572872 | tf_op jit(solution)/shard_map/ppermute | solution.py:21
  365.7 7.3 copy-start.111
  365.7 9.3 copy-start.38
  380.3 9.7 slice-start.2
  381.5 8.4 copy-start.74
  381.5 8.5 slice-start.3
  403.2 287.3 %reduce-scatter.5.cloned.1.call-start = ((), (), s32[]{:S(2)}) async-start(), calls=%async_computation.10 | async-start | bytes 3379200 | tf_op jit(solution)/shard_map/reduce_scatter | solution.py:147
  416.4 24.4 %collective-permute-start.4 = (bf16[512,512]{0,1:T(8,128)(2,1)S(1)}, bf16[512,512]{0,1:T(8,128)(2,1)S(1)}, u32[]{:S(2)}, u32[]{:S(2)}) collective-permute-start(bf16[512,512]{0,1:T(8,128)(2,1)S(1)} %fusion.130), channel_id=1, source_target_pairs={{0,16},{16,0},{1,17},{17,1},{2,18},{18,2},{3,19},{19,3},{4,20},{20... | collective-permute-start | bytes 1572872 | tf_op jit(solution)/shard_map/ppermute | solution.py:21
  427.2 14.0 %copy-start.109 = (f32[128]{0:T(128)S(1)}, f32[128]{0:T(128)}, u32[]{:S(2)}) copy-start(f32[128]{0:T(128)} %multiply_exponential_fusion.1) | copy-start | bytes 1540
  427.2 15.2 %copy-start.36 = (bf16[512,512]{0,1:T(8,128)(2,1)S(1)}, bf16[512,512]{0,1:T(8,128)(2,1)}, u32[]{:S(2)}) copy-start(bf16[512,512]{0,1:T(8,128)(2,1)} %copy-done.35) | copy-start | bytes 1572868
  427.2 15.2 %copy-start.87 = (f32[512]{0:T(512)S(1)}, f32[512]{0:T(512)}, u32[]{:S(2)}) copy-start(f32[512]{0:T(512)} %copy-done.86) | copy-start | bytes 6148
  427.2 15.2 %copy-start.97 = (f32[1,256]{1,0:T(1,128)S(1)}, f32[1,256]{1,0:T(1,128)}, u32[]{:S(2)}) copy-start(f32[1,256]{1,0:T(1,128)} %copy-done.96) | copy-start | bytes 3076
  449.8 6.1 copy-start.17
  449.8 364.7 %reduce-scatter.11.cloned.1.call-start = ((), (), s32[]{:S(2)}) async-start(), calls=%async_computation.13 | async-start | bytes 8110080 | tf_op jit(solution)/shard_map/reduce_scatter | solution.py:147
  480.5 462.2 %reduce-scatter.7.cloned.1.call-start = ((), (), s32[]{:S(2)}) async-start(), calls=%async_computation.11 | async-start | bytes 8110080 | tf_op jit(solution)/shard_map/reduce_scatter | solution.py:147
  519.2 468.4 %all-to-all-start.1 = ((bf16[8,128,640]{2,1,0:T(8,128)(2,1)}), bf16[8,128,640]{2,1,0:T(8,128)(2,1)S(1)}, u32[]{:S(2)}, u32[]{:S(2)}) async-start(bf16[8,128,640]{2,1,0:T(8,128)(2,1)} %bitcast.78), calls=%async_computation.1 | async-start | bytes 2621440 | tf_op jit(solution)/shard_map/all_to_all | solution.py:229
  944.4 49.4 %collective-permute-start.5 = (bf16[80,2176]{1,0:T(8,128)(2,1)}, bf16[80,2176]{1,0:T(8,128)(2,1)}, u32[]{:S(2)}, u32[]{:S(2)}) collective-permute-start(bf16[80,2176]{1,0:T(8,128)(2,1)} %broadcast_select_fusion.2), channel_id=1, source_target_pairs={{0,16},{16,0},{1,17},{17,1},{2,18},{18,2},{3,19},{19,3},{4,20},{20... | collective-permute-start | bytes 1044488 | tf_op jit(solution)/shard_map/ppermute | solution.py:21
  (99 other events, 257.9 us)
Sparse Core Ops, SparseCore 0:
  23.9 73.6 all-gather.5
  100.9 58.2 all-gather.9
  162.7 74.3 all-gather.7
  239.8 75.7 all-gather.11
  403.4 146.1 reduce-scatter.8
  551.8 138.6 reduce-scatter.4
  696.2 118.3 reduce-scatter.10
  821.2 121.4 reduce-scatter.6

commit v2 on v1

--- a/solution.py
+++ b/solution.py
@@ -1,6 +1,8 @@
 import jax
 import jax.numpy as jnp
 from jax import lax
+from jax.experimental import pallas as pl
+from jax.experimental.pallas import tpu as pltpu
 from jax.sharding import PartitionSpec as P
 
 HD = 256
@@ -40,6 +42,49 @@
 
 def gated(gate, up):
     return jax.nn.gelu(gate, approximate=True) * up
+
+
+def grads_kernel(normed, normed_ff, d_branch, d_branch_ff, d_query, d_keyval, mixed, d_gateup,
+                 hidden, out):
+    at = 0
+    for left, right in (
+        (normed, d_query.at[0]), (normed, d_keyval), (d_branch, mixed.at[0]),
+        (normed_ff, d_gateup.at[0]), (d_branch_ff, hidden.at[0]),
+    ):
+        size = right.shape[1]
+        product = lax.dot_general(
+            left[...], right[...], (((0,), (0,)), ((), ())), preferred_element_type=F32
+        )
+        out[0, :, at : at + size] = product.astype(BF)
+        at += size
+
+
+def packed_grads(normed, normed_ff, d_branch, d_branch_ff, d_query, d_keyval, mixed, d_gateup,
+                 hidden):
+    parts, length = d_query.shape[:2]
+    width = normed.shape[1]
+    kv = d_keyval.shape[1] // parts
+    columns = d_query.shape[2] + kv + mixed.shape[2] + d_gateup.shape[2] + hidden.shape[2]
+    shared = pl.BlockSpec((length, width), lambda t: (0, 0))
+
+    def own(array):
+        return pl.BlockSpec((1, length, array.shape[2]), lambda t: (t, 0, 0))
+
+    return pl.pallas_call(
+        grads_kernel,
+        grid=(parts,),
+        out_shape=jax.ShapeDtypeStruct((parts, width, columns), BF),
+        in_specs=[shared] * 4
+        + [own(d_query), pl.BlockSpec((length, kv), lambda t: (0, t))]
+        + [own(mixed), own(d_gateup), own(hidden)],
+        out_specs=pl.BlockSpec((1, width, columns), lambda t: (t, 0, 0)),
+        compiler_params=pltpu.CompilerParams(vmem_limit_bytes=40 * 1024 * 1024),
+        cost_estimate=pl.CostEstimate(
+            flops=2 * parts * length * width * columns,
+            bytes_accessed=2 * parts * columns * (width + length) + 8 * length * width,
+            transcendentals=0,
+        ),
+    )(normed, normed_ff, d_branch, d_branch_ff, d_query, d_keyval, mixed, d_gateup, hidden)
 
 
 def layer_forward(rows, attn_weights, ff_weights, gains, qk_gain, tables, mask):
@@ -85,13 +130,10 @@
     d_branch_ff, dg3 = pull(grad_output)
     d_branch_ff = d_branch_ff.astype(BF)
     d_hidden = dots("ld,tdf->tlf", d_branch_ff, w_down)
-    g_down = dots("ld,tlf->tdf", d_branch_ff, hidden).astype(BF)
     half = gateup.shape[-1] // 2
     _, pull = jax.vjp(gated, gateup[..., :half], gateup[..., half:])
     d_gate, d_up = pull(d_hidden)
     d_gateup = jnp.concatenate([d_gate.astype(BF), d_up.astype(BF)], axis=-1)
-    g_gateup = dots("ld,tlc->tdc", normed_ff, d_gateup).astype(BF)
-    ff_share = scatter_total((g_gateup, g_down))
     d_normed_ff = dots("tlc,tdc->ld", d_gateup, w_gateup)
     _, pull = jax.vjp(rms_scale, middle, gains[2])
     d_middle, dg2 = pull(d_normed_ff)
@@ -100,7 +142,6 @@
     d_branch, dg1 = pull(d_middle)
     d_branch = d_branch.astype(BF)
     d_mixed = dots("qd,hde->hqe", d_branch, w_out).astype(BF)
-    g_out = dots("qd,hqe->hde", d_branch, mixed).astype(BF)
     d_probs = dots("hqd,kd->hqk", d_mixed, values)
     wide = probs.astype(F32)
     inner = jnp.sum(wide * d_probs, axis=-1, keepdims=True)
@@ -118,16 +159,16 @@
     _, pull = jax.vjp(lambda raw, gain: rotated(raw, gain, tables), keys_raw, qk_gain[1])
     d_keys_raw, dgk = pull(d_both[:, :HD])
     d_keyval = jnp.concatenate([d_keys_raw, d_both[:, HD:]], axis=1).astype(BF)
+    packed = packed_grads(
+        normed, normed_ff, d_branch, d_branch_ff, d_query_raw, d_keyval, mixed, d_gateup, hidden
+    )
     d_keyval = d_keyval.reshape(length, parts, 2 * HD // parts)
-    g_query = dots("ld,tlc->tdc", normed, d_query_raw).astype(BF)
-    g_keyval = dots("ld,ltc->tdc", normed, d_keyval).astype(BF)
-    attn_share = scatter_total((g_query, g_keyval, g_out))
     d_normed = dots("tlc,tdc->ld", d_query_raw, w_query) + dots("ltc,tdc->ld", d_keyval, w_keyval)
     _, pull = jax.vjp(rms_scale, rows, gains[0])
     d_rows, dg0 = pull(d_normed)
     d_rows = d_rows + d_middle
     small = jnp.concatenate([dg0, dg1, dg2, dg3, dgq, dgk])
-    return d_rows, attn_share, ff_share, small
+    return d_rows, packed, small
 
 
 def gathered(shard, widths):
@@ -141,8 +182,7 @@
     return tuple(pieces)
 
 
-def scatter_total(grads):
-    packed = jnp.concatenate(grads, axis=2)
+def scatter_total(packed):
     packed = packed.reshape(packed.shape[0] * packed.shape[1], packed.shape[2])
     return lax.psum_scatter(packed, EVERY, scatter_dimension=0, tiled=True)
 
@@ -168,12 +208,11 @@
     mine = jnp.where(first, top, bottom)
     other = swap(jnp.where(first, bottom, top))
     layers = (jnp.where(first, mine, other), jnp.where(first, other, mine))
-    cut = attn.shape[1]
-    attn_w = [None, None]
-    ff_w = [None, None]
-    for index in range(2):
-        attn_w[index] = gathered(layers[index][:, :cut], attn_widths)
-        ff_w[index] = gathered(layers[index][:, cut:], ff_widths)
+    first_w = gathered(layers[0], attn_widths + ff_widths)
+    second_shard, _ = lax.optimization_barrier((layers[1], first_w[0]))
+    second_w = gathered(second_shard, attn_widths + ff_widths)
+    attn_w = (first_w[:3], second_w[:3])
+    ff_w = (first_w[3:], second_w[3:])
 
     gains = lax.all_gather(
         jnp.concatenate([norm_gains[0].reshape(-1), qk_gains[0].reshape(-1)]), "section", axis=0
@@ -218,14 +257,18 @@
     shares = [None, None]
     smalls = [None, None]
     for index in (1, 0):
-        grad_rows, attn_share, ff_share, smalls[index] = layer_backward(
+        grad_rows, packed_grad, smalls[index] = layer_backward(
             kept[index], attn_w[index], ff_w[index], norm_all[index], qk_all[index],
             tables[index], grad,
         )
-        shares[index] = jnp.concatenate([attn_share, ff_share], axis=1)
         grad = grad_rows.astype(BF).astype(F32)
-
-    back = jnp.stack([grad_rows.astype(BF), output.astype(BF)]).reshape(2 * micro, part, width)
+        if index == 1:
+            grad, packed_grad = lax.optimization_barrier((grad, packed_grad))
+        shares[index] = scatter_total(packed_grad)
+
+    small = lax.psum(jnp.stack(smalls), ("section", "dp", "tensor"))
+    sending, small = lax.optimization_barrier((grad_rows.astype(BF), small))
+    back = jnp.stack([sending, output.astype(BF)]).reshape(2 * micro, part, width)
     back = lax.all_to_all(back, ("section", "tensor"), 0, 0, tiled=True)
     ends = back.reshape(2, micro, part, width).transpose(1, 0, 2, 3).reshape(micro, span, width)
     ends = ends.astype(F32)[None, :, :, None]
@@ -239,7 +282,6 @@
     for size in attn_widths + ff_widths:
         found.append(grads[:, at : at + size])
         at += size
-    small = lax.psum(jnp.stack(smalls), ("section", "dp", "tensor"))
     small = lax.dynamic_index_in_dim(small, section, 0, keepdims=False)
     return (
         ends,

time: 1010 us -> 929 us (0.920)
  local copies, waits for them, and re-layouts: 84.6 us -> 41.4 us
  matrix products: 128 us -> 95.1 us
  Pallas kernels: 0 us -> 17.3 us
  waiting for transfers between devices: 623 us -> 606 us
  other arithmetic: 82.8 us -> 71.3 us
    dot_general x41 -> x31, matrix products: 128 us -> 94.5 us  [dots(): return jnp.einsum(pattern, left, right, preferred_element_type=F32)]
    concatenate x6 -> x0, local copies, waits for them, and re-layouts: 30.6 us -> none  [the longest x4 28.7 us: scatter_total(): packed = jnp.concatenate(grads, axis=2)]
    reduce_scatter x4 -> x2, waiting for transfers between devices: 416 us -> 396 us  [scatter_total(): return lax.psum_scatter(packed, EVERY, scatter_dimension=0, tiled=True)]
    pallas_call x0 -> x2, Pallas kernels: none -> 17.3 us  [packed_grads(): pl.pallas_call(grads_kernel, grid=(parts,), out_shape=jax.ShapeDtypeStruc...]
    concatenate x4, other arithmetic: 16.4 us -> 1.29 us  [the longest x2 1.22 us: layer_backward(): d_gateup = jnp.concatenate([d_gate.astype(BF), d_up.astype(BF)], axis=-1)]
    unnamed x282 -> x280, local copies, waits for them, and re-layouts: 36.6 us -> 26.9 us
    all_gather x4 -> x2, waiting for transfers between devices: 147 us -> 138 us  [gathered(): whole = lax.all_gather(shard, EVERY, axis=0, tiled=True)]
  transfers between devices with their start and end apart: 16 -> 12, of which waited for: 13 -> 10; matrix products, arithmetic and copies ran while one was open for 19% -> 8% of each run, Pallas kernels for 0% -> 1%
where the time goes in v2:
time: 929 us; the launch traced here: 919 us
  waiting for transfers between devices  606 us (65%)
  matrix products  95.1 us (10%)
  other arithmetic  71.3 us (8%)
  blocking collectives  50.9 us (5%)
  local copies, waits for them, and re-layouts  41.4 us (4%)
  starting transfers between devices  20.4 us (2%)
  Pallas kernels  17.3 us (2%)
  between operations  16.5 us (2%)
    reduce_scatter x2, waiting for transfers between devices, scatter_total(): return lax.psum_scatter(packed, EVERY, scatter_dimension=0, tiled=True)  396 us
    all_gather x2, waiting for transfers between devices, gathered(): whole = lax.all_gather(shard, EVERY, axis=0, tiled=True)  138 us
    dot_general x31, matrix products, dots(): return jnp.einsum(pattern, left, right, preferred_element_type=F32)  94.5 us
    ppermute x6, waiting for transfers between devices, swap(): return lax.ppermute(array, 'section', [(0, 1), (1, 0)])  46.2 us
    psum x1, blocking collectives, body(): small = lax.psum(jnp.stack(smalls), ('section', 'dp', 'tensor'))  41 us
    unnamed x280, local copies, waits for them, and re-layouts  26.9 us
    all_to_all x1, waiting for transfers between devices, body(): came = lax.all_to_all(sent, ('section', 'tensor'), 0, 0, tiled=True)  23.8 us
    sub x2, other arithmetic, layer_forward(): weights = jnp.exp(scores - peak)  19.7 us
  transfers between devices with their start and end apart: 12, of which 10 were waited for; matrix products, arithmetic and copies ran while one was open for 8% of the time, Pallas kernels for 1%

profile of v2, /device:TPU:0, one launch (start us, length us, event | category | flops | bytes accessed | tf_op | source)
XLA Modules:
  0.0 918.6 jit_solution(17975735662751863501)
XLA Ops:
  11.9 3.0 collective-permute-start
  14.9 8.1 collective-permute-done
  26.0 6.1 all-to-all-start
  32.2 9.8 %all-gather = f32[6144]{0:T(1024)S(1)} all-gather(f32[3072]{0:T(1024)S(1)} %pad_maximum_fusion.19), channel_id=2, replica_groups=mesh['section'=2,'dp'=4,'tensor'=4] {'section'}, dimensions={0}, use_global_device_ids=true | all-gather | bytes 36864 | tf_op jit(solution)/shard_map/all_gather | solution.py:217
  45.2 1.9 fusion.58
  47.1 23.8 %all-to-all-done = bf16[8,128,640]{2,1,0:T(8,128)(2,1)S(1)} async-done(((bf16[8,128,640]{2,1,0:T(8,128)(2,1)}), bf16[8,128,640]{2,1,0:T(8,128)(2,1)S(1)}, u32[]{:S(2)}, u32[]{:S(2)}) %all-to-all-start) | async-done | bytes 1310752 | tf_op jit(solution)/shard_map/all_to_all | solution.py:226
  72.6 57.6 %all-gather.4.cloned.1.call-done = bf16[2560,2176]{1,0:T(8,128)(2,1)} async-done(((bf16[80,2176]{1,0:T(8,128)(2,1)}), bf16[2560,2176]{1,0:T(8,128)(2,1)}) %all-gather.4.cloned.1.call-update) | async-done | bytes 11141136 | tf_op jit(solution)/shard_map/all_gather | solution.py:176
  137.9 3.7 fusion.56
  142.2 80.9 %all-gather.6.cloned.1.call-done = bf16[2560,2176]{1,0:T(8,128)(2,1)} async-done(((bf16[80,2176]{1,0:T(8,128)(2,1)}), bf16[2560,2176]{1,0:T(8,128)(2,1)}) %all-gather.6.cloned.1.call-update) | async-done | bytes 11141136 | tf_op jit(solution)/shard_map/all_gather | solution.py:176
  225.3 1.9 fusion.60
  229.1 4.6 fusion.124
  233.7 9.9 %fusion.210 = (f32[4,512]{1,0:T(4,128)S(1)}, f32[4,512,1024]{2,1,0:T(8,128)S(1)}) fusion(f32[4,512,1024]{2,1,0:T(8,128)} %fusion.124, pred[512,1024]{1,0:T(8,128)(4,1)S(1)} %copy-done.62), kind=kOutput, calls=%fused_computation.428 | output fusion | flops 12583935 | bytes 17309696 | tf_op jit(solution)/shard_map/sub | solution.py:106
  245.0 2.9 copy-done.8
  255.1 3.4 fusion.38
  260.1 1.8 copy-done.27
  261.9 1.9 multiply_reduce_fusion.15
  264.9 3.7 fusion.54
  273.7 12.0 %collective-permute-done.2 = bf16[512,512]{1,0:T(8,128)(2,1)S(1)} collective-permute-done((bf16[512,512]{1,0:T(8,128)(2,1)S(1)}, bf16[512,512]{1,0:T(8,128)(2,1)S(1)}, u32[]{:S(2)}, u32[]{:S(2)}) %collective-permute-start.2) | collective-permute-done | bytes 524320 | tf_op jit(solution)/shard_map/ppermute | solution.py:23
  285.7 4.6 fusion.123
  290.3 9.7 %fusion.211 = (f32[4,512]{1,0:T(4,128)S(1)}, f32[4,512,1024]{2,1,0:T(8,128)S(1)}) fusion(f32[4,512,1024]{2,1,0:T(8,128)} %fusion.123, pred[512,1024]{1,0:T(8,128)(4,1)S(1)} %copy-done.61), kind=kOutput, calls=%fused_computation.429 | output fusion | flops 12583935 | bytes 17309696 | tf_op jit(solution)/shard_map/sub | solution.py:106
  302.5 2.6 multiply_reduce_fusion.14
  305.9 5.4 fusion.41
  311.3 1.9 multiply_convert_fusion.hidden
  313.2 3.7 multiply_reduce_fusion.12
  319.3 6.9 fusion.29
  326.2 9.0 multiply_reduce_fusion.2
  335.2 2.7 multiply_reduce_fusion.3
  338.3 2.5 fusion.78
  342.1 3.8 fusion.4
  345.9 2.8 fusion.5
  348.7 3.6 fusion.81
  359.1 2.3 convolution_bitcast_fusion.3
  361.5 5.6 collective-permute-done.3
  369.2 1.9 fusion.85
  371.2 8.7 shard_map.152
  380.9 1.8 multiply_reduce_fusion.4
  383.2 7.7 fusion.22
  391.0 3.5 multiply_reduce_fusion.5
  413.0 17.4 %collective-permute-done.4 = bf16[512,512]{1,0:T(8,128)(2,1)S(1)} collective-permute-done((bf16[512,512]{1,0:T(8,128)(2,1)S(1)}, bf16[512,512]{1,0:T(8,128)(2,1)S(1)}, u32[]{:S(2)}, u32[]{:S(2)}) %collective-permute-start.4) | collective-permute-done | bytes 524320 | tf_op jit(solution)/shard_map/ppermute | solution.py:23
  433.2 8.6 shard_map.153
  445.5 3.5 fusion.102
  449.1 41.0 %psum.7 = f32[2,3072]{1,0:T(2,128)S(1)} all-reduce(f32[2,3072]{1,0:T(2,128)S(1)} %pad_maximum_fusion.18), channel_id=1, replica_groups=mesh['section'=2,'dp'=4,'tensor'=4] {'section','dp','tensor'}, use_global_device_ids=true, to_apply=%region_44.45 | all-reduce | flops 6144 | bytes 49152 | tf_op jit(solution)/shard_map/psum | solution.py:269
  490.2 2.1 fusion.95
  493.5 4.9 all-to-all-start.1
  498.4 150.1 %reduce-scatter.5.cloned.1.call-done = bf16[80,2176]{1,0:T(8,128)(2,1)} async-done(((bf16[2560,2176]{1,0:T(8,128)(2,1)}), bf16[80,2176]{1,0:T(8,128)(2,1)}) %reduce-scatter.5.cloned.1.call-update) | async-done | bytes 348176 | tf_op jit(solution)/shard_map/reduce_scatter | solution.py:187
  648.5 246.3 %reduce-scatter.3.cloned.1.call-done = bf16[80,2176]{1,0:T(8,128)(2,1)} async-done(((bf16[2560,2176]{1,0:T(8,128)(2,1)}), bf16[80,2176]{1,0:T(8,128)(2,1)}) %reduce-scatter.3.cloned.1.call-update) | async-done | bytes 348176 | tf_op jit(solution)/shard_map/reduce_scatter | solution.py:187
  900.1 3.6 reshape.671
  903.7 3.0 collective-permute-done.5
  (439 shorter events, 93.4 us)
Async XLA Ops:
  7.2 123.1 %all-gather.4.cloned.1.call-start = ((), (), s32[]{:S(2)}) async-start(), calls=%async_computation.4 | async-start | bytes 11489280 | tf_op jit(solution)/shard_map/all_gather | solution.py:176
  10.8 14.0 %copy-start.60 = (bf16[1,4,256,1,640]{4,2,3,1,0:T(8,128)(2,1)S(1)}, bf16[1,4,256,1,640]{4,2,3,1,0:T(8,128)(2,1)}, u32[]{:S(2)}) copy-start(bf16[1,4,256,1,640]{4,2,3,1,0:T(8,128)(2,1)} %param.9) | copy-start | bytes 3932164
  11.9 11.2 %collective-permute-start = (bf16[80,2176]{1,0:T(8,128)(2,1)S(1)}, bf16[80,2176]{1,0:T(8,128)(2,1)S(1)}, u32[]{:S(2)}, u32[]{:S(2)}) collective-permute-start(bf16[80,2176]{1,0:T(8,128)(2,1)S(1)} %broadcast_select_fusion.6), channel_id=1, source_target_pairs={{0,16},{16,0},{1,17},{17,1},{2,18},{18,2},{3,19},{19,3},{4,20},{20... | collective-permute-start | bytes 1044488 | tf_op jit(solution)/shard_map/ppermute | solution.py:23
  24.0 199.0 %all-gather.6.cloned.1.call-start = ((), (), s32[]{:S(2)}) async-start(), calls=%async_computation.5 | async-start | bytes 11489280 | tf_op jit(solution)/shard_map/all_gather | solution.py:176
  24.8 7.3 copy-start.111
  24.8 7.3 copy-start.121
  26.0 44.9 %all-to-all-start = ((bf16[8,128,640]{2,1,0:T(8,128)(2,1)}), bf16[8,128,640]{2,1,0:T(8,128)(2,1)S(1)}, u32[]{:S(2)}, u32[]{:S(2)}) async-start(bf16[8,128,640]{2,1,0:T(8,128)(2,1)} %bitcast.16), calls=%async_computation | async-start | bytes 2621440 | tf_op jit(solution)/shard_map/all_to_all | solution.py:226
  32.0 616.4 %reduce-scatter.5.cloned.1.call-start = ((), (), s32[]{:S(2)}) async-start(), calls=%async_computation.7 | async-start | bytes 11489280 | tf_op jit(solution)/shard_map/reduce_scatter | solution.py:187
  43.4 91.7 %copy-start.68 = (f32[512]{0:T(512)}, f32[512]{0:T(512)S(1)}, u32[]{:S(2)}) copy-start(f32[512]{0:T(512)S(1)} %convert_element_type.194) | copy-start | bytes 6148
  43.4 91.7 %copy-start.117 = (f32[128]{0:T(128)}, f32[128]{0:T(128)S(1)}, u32[]{:S(2)}) copy-start(f32[128]{0:T(128)S(1)} %multiply_exponential_fusion.1) | copy-start | bytes 1540
  44.6 27.8 %copy-start.65 = (f32[640]{0:T(1024)}, f32[640]{0:T(1024)S(1)}, u32[]{:S(2)}) copy-start(f32[640]{0:T(1024)S(1)} %get-tuple-element.49) | copy-start | bytes 7684
  45.2 89.2 %copy-start.102 = (f32[1,256]{1,0:T(1,128)}, f32[1,256]{1,0:T(1,128)S(1)}, u32[]{:S(2)}) copy-start(f32[1,256]{1,0:T(1,128)S(1)} %get-tuple-element.92) | copy-start | bytes 3076
  70.9 182.9 %copy-start.12 = (bf16[8,128,640]{2,1,0:T(8,128)(2,1)}, bf16[8,128,640]{2,1,0:T(8,128)(2,1)S(1)}, u32[]{:S(2)}) copy-start(bf16[8,128,640]{2,1,0:T(8,128)(2,1)S(1)} %all-to-all-done) | copy-start | bytes 3932164
  72.1 60.4 %copy-start.82 = (f32[4,128]{1,0:T(4,128)}, f32[4,128]{1,0:T(4,128)S(1)}, u32[]{:S(2)}) copy-start(f32[4,128]{1,0:T(4,128)S(1)} %fusion.103) | copy-start | bytes 6148
  72.2 60.3 %copy-start.88 = (f32[512]{0:T(512)}, f32[512]{0:T(512)S(1)}, u32[]{:S(2)}) copy-start(f32[512]{0:T(512)S(1)} %bitcast_rsqrt_fusion) | copy-start | bytes 6148
  72.6 65.3 %copy-start.2 = (bf16[512,640]{1,0:T(8,128)(2,1)}, bf16[512,640]{1,0:T(8,128)(2,1)S(1)}, u32[]{:S(2)}) copy-start(bf16[512,640]{1,0:T(8,128)(2,1)S(1)} %fusion.101.normed) | copy-start | bytes 1966084
  136.4 90.9 %copy-start.39 = (f32[512,128]{1,0:T(8,128)}, f32[512,128]{1,0:T(8,128)S(1)}, u32[]{:S(2)}) copy-start(f32[512,128]{1,0:T(8,128)S(1)} %get-tuple-element.102) | copy-start | bytes 786436
  136.4 90.9 %copy-start.41 = (f32[512,128]{1,0:T(8,128)}, f32[512,128]{1,0:T(8,128)S(1)}, u32[]{:S(2)}) copy-start(f32[512,128]{1,0:T(8,128)S(1)} %get-tuple-element.103) | copy-start | bytes 786436
  136.4 91.1 %collective-permute-start.1 = (bf16[512,512]{1,0:T(8,128)(2,1)S(1)}, bf16[512,512]{1,0:T(8,128)(2,1)}, u32[]{:S(2)}, u32[]{:S(2)}) collective-permute-start(bf16[512,512]{1,0:T(8,128)(2,1)S(1)} %pad_maximum_fusion.13), channel_id=1, source_target_pairs={{0,16},{16,0},{1,17},{17,1},{2,18},{18,2},{3,19},{19,3},{4,20},{20... | collective-permute-start | bytes 1572872 | tf_op jit(solution)/shard_map/ppermute | solution.py:23
  142.2 85.0 %copy-start.63 = (f32[4,512]{1,0:T(4,128)}, f32[4,512]{1,0:T(4,128)S(1)}, u32[]{:S(2)}) copy-start(f32[4,512]{1,0:T(4,128)S(1)} %fusion.184) | copy-start | bytes 24580
  229.1 15.9 %copy-start.29 = (bf16[1024,512]{1,0:T(8,128)(2,1)}, bf16[1024,512]{1,0:T(8,128)(2,1)S(1)}, u32[]{:S(2)}) copy-start(bf16[1024,512]{1,0:T(8,128)(2,1)S(1)} %pad_maximum_fusion.6) | copy-start | bytes 3145732
  243.7 8.0 slice-start.3
  264.4 104.8 %copy-start.24 = (bf16[512,640]{1,0:T(8,128)(2,1)}, bf16[512,640]{1,0:T(8,128)(2,1)S(1)}, u32[]{:S(2)}) copy-start(bf16[512,640]{1,0:T(8,128)(2,1)S(1)} %get-tuple-element.55) | copy-start | bytes 1966084
  271.4 14.2 %collective-permute-start.2 = (bf16[512,512]{1,0:T(8,128)(2,1)S(1)}, bf16[512,512]{1,0:T(8,128)(2,1)S(1)}, u32[]{:S(2)}, u32[]{:S(2)}) collective-permute-start(bf16[512,512]{1,0:T(8,128)(2,1)S(1)} %pad_maximum_fusion.14), channel_id=1, source_target_pairs={{0,16},{16,0},{1,17},{17,1},{2,18},{18,2},{3,19},{19,3},{4,20},{20... | collective-permute-start | bytes 1572872 | tf_op jit(solution)/shard_map/ppermute | solution.py:23
  273.6 16.7 %copy-start.49 = (bf16[4,512,128]{2,1,0:T(8,128)(2,1)}, bf16[4,512,128]{2,1,0:T(8,128)(2,1)S(1)}, u32[]{:S(2)}) copy-start(bf16[4,512,128]{2,1,0:T(8,128)(2,1)S(1)} %get-tuple-element.68) | copy-start | bytes 1572868
  273.6 16.7 %copy-start.51 = (bf16[4,512,128]{2,1,0:T(8,128)(2,1)}, bf16[4,512,128]{2,1,0:T(8,128)(2,1)S(1)}, u32[]{:S(2)}) copy-start(bf16[4,512,128]{2,1,0:T(8,128)(2,1)S(1)} %get-tuple-element.69) | copy-start | bytes 1572868
  285.7 15.5 %copy-start.31 = (bf16[1024,512]{1,0:T(8,128)(2,1)}, bf16[1024,512]{1,0:T(8,128)(2,1)S(1)}, u32[]{:S(2)}) copy-start(bf16[1024,512]{1,0:T(8,128)(2,1)S(1)} %pad_maximum_fusion.8) | copy-start | bytes 3145732
  301.2 39.6 %copy-start.11 = (bf16[4,512,1024]{2,1,0:T(8,128)(2,1)}, bf16[4,512,1024]{2,1,0:T(8,128)(2,1)S(1)}, u32[]{:S(2)}) copy-start(bf16[4,512,1024]{2,1,0:T(8,128)(2,1)S(1)} %divide_convert_fusion) | copy-start | bytes 12582916
  326.2 9.0 copy-start.53
  353.8 13.3 %collective-permute-start.3 = (bf16[512,512]{1,0:T(8,128)(2,1)S(1)}, bf16[512,512]{1,0:T(8,128)(2,1)S(1)}, u32[]{:S(2)}, u32[]{:S(2)}) collective-permute-start(bf16[512,512]{1,0:T(8,128)(2,1)S(1)} %fusion.122), channel_id=1, source_target_pairs={{0,16},{16,0},{1,17},{17,1},{2,18},{18,2},{3,19},{19,3},{4,20},{20... | collective-permute-start | bytes 1572872 | tf_op jit(solution)/shard_map/ppermute | solution.py:23
  371.1 8.7 copy-start.22
  371.2 8.7 copy-start.25
  371.2 8.7 copy-start.71
  380.3 514.5 %reduce-scatter.3.cloned.1.call-start = ((), (), s32[]{:S(2)}) async-start(), calls=%async_computation.6 | async-start | bytes 11489280 | tf_op jit(solution)/shard_map/reduce_scatter | solution.py:187
  380.9 10.0 %slice-start.5 = ((s8[11141120]{0:T(1024)(128)(4,1)}), s8[4194304]{0:T(1024)(128)(4,1)S(1)}, s32[]{:S(2)}) async-start(s8[11141120]{0:T(1024)(128)(4,1)} %bitcast.307), calls=%async_computation.13 | async-start | bytes 8388608
  383.1 7.8 slice-start.6
  383.1 7.8 slice-start.7
  383.1 7.8 copy-start.75
  383.1 7.8 copy-start.91
  405.0 25.4 %collective-permute-start.4 = (bf16[512,512]{1,0:T(8,128)(2,1)S(1)}, bf16[512,512]{1,0:T(8,128)(2,1)S(1)}, u32[]{:S(2)}, u32[]{:S(2)}) collective-permute-start(bf16[512,512]{1,0:T(8,128)(2,1)S(1)} %fusion.121), channel_id=1, source_target_pairs={{0,16},{16,0},{1,17},{17,1},{2,18},{18,2},{3,19},{19,3},{4,20},{20... | collective-permute-start | bytes 1572872 | tf_op jit(solution)/shard_map/ppermute | solution.py:23
  413.0 17.7 %copy-start.118 = (f32[128]{0:T(128)S(1)}, f32[128]{0:T(128)}, u32[]{:S(2)}) copy-start(f32[128]{0:T(128)} %copy-done.117) | copy-start | bytes 1540
  413.0 18.9 %copy-start.36 = (bf16[512,512]{1,0:T(8,128)(2,1)S(1)}, bf16[512,512]{1,0:T(8,128)(2,1)}, u32[]{:S(2)}) copy-start(bf16[512,512]{1,0:T(8,128)(2,1)} %copy-done.35) | copy-start | bytes 1572868
  413.0 18.9 %copy-start.77 = (f32[512]{0:T(512)S(1)}, f32[512]{0:T(512)}, u32[]{:S(2)}) copy-start(f32[512]{0:T(512)} %copy-done.76) | copy-start | bytes 6148
  413.0 18.9 %copy-start.103 = (f32[1,256]{1,0:T(1,128)S(1)}, f32[1,256]{1,0:T(1,128)}, u32[]{:S(2)}) copy-start(f32[1,256]{1,0:T(1,128)} %copy-done.102) | copy-start | bytes 3076
  445.5 44.7 %copy-start.83 = (f32[4,128]{1,0:T(4,128)S(1)}, f32[4,128]{1,0:T(4,128)}, u32[]{:S(2)}) copy-start(f32[4,128]{1,0:T(4,128)} %copy-done.82) | copy-start | bytes 6148
  449.0 43.3 %copy-start.37 = (bf16[1,512,640]{2,1,0:T(8,128)(2,1)S(1)}, bf16[1,512,640]{2,1,0:T(8,128)(2,1)}, u32[]{:S(2)}) copy-start(bf16[1,512,640]{2,1,0:T(8,128)(2,1)} %get-tuple-element.73) | copy-start | bytes 1966084
  493.5 404.0 %all-to-all-start.1 = ((bf16[8,128,640]{2,1,0:T(8,128)(2,1)}), bf16[8,128,640]{2,1,0:T(8,128)(2,1)S(1)}, u32[]{:S(2)}, u32[]{:S(2)}) async-start(bf16[8,128,640]{2,1,0:T(8,128)(2,1)} %bitcast.71), calls=%async_computation.1 | async-start | bytes 2621440 | tf_op jit(solution)/shard_map/all_to_all | solution.py:272
  895.8 10.9 %collective-permute-start.5 = (bf16[80,2176]{1,0:T(8,128)(2,1)S(1)}, bf16[80,2176]{1,0:T(8,128)(2,1)}, u32[]{:S(2)}, u32[]{:S(2)}) collective-permute-start(bf16[80,2176]{1,0:T(8,128)(2,1)S(1)} %broadcast_select_fusion.2), channel_id=1, source_target_pairs={{0,16},{16,0},{1,17},{17,1},{2,18},{18,2},{3,19},{19,3},{4,20},{20... | collective-permute-start | bytes 1044488 | tf_op jit(solution)/shard_map/ppermute | solution.py:23
  (94 other events, 231.2 us)
Sparse Core Ops, SparseCore 0:
  24.1 106.0 all-gather.3
  133.1 89.9 all-gather.5
  380.4 267.9 reduce-scatter.4
  650.6 244.1 reduce-scatter.2
